TPU v7x, 32 devices: a whole 2x2x4 slice. The times are simulated.
32 devices in a mesh: ctx: 8 (over y, x, core), ch: 4 (over z).
Axes of the slice: x: 2, y: 2, z: 4, core: 2. Of those that a mesh axis runs over, the one named last changes fastest.
Arguments:
- gate_input: bfloat16 [8192, 4096], P('ch', 'ctx'), may hold values from -90 to 90
- key_input: bfloat16 [8192, 4096], P('ch', 'ctx'), may hold values from -6 to 6
- value_input: bfloat16 [8192, 4096], P('ch', 'ctx'), may hold values from -6 to 6
- short_filter: float32 [3, 3, 8192], P(None, None, 'ch'), may hold values from -3.5 to 3.5
- mr_filter: float32 [512, 128], P('ch'), may hold values from -0.5 to 0.5
- mr_skip: float32 [8192], P('ch'), may hold values from -3 to 3
- norm_gain: float32 [8192], P('ch'), may hold values from 0.5 to 1.5
- doc_lengths: int32 [16], replicated, may hold values from 1 to 2048, 4096 in all
Outputs:
- relaid: bfloat16 [8192, 4096], P(('ch', 'ctx'))
Inputs may be any that keep to these rules, and one draw needn't show every extreme that they name: `doc_lengths`: the 16 lengths sum to 4096, and one of them is exactly 2048.
All inputs are finite; a program needn't handle non-finite values.
Results may differ from a plain program's by a relative error of at most 0.0095.
Values may be sent and summed in bfloat16 or wider, within the bound.
A program may use at most 128 MiB of HBM per device.

v0:
```python
import math

import jax
import jax.numpy as jnp
from jax import lax
from jax.sharding import PartitionSpec as P

D = 8192
GROUP = 16
SHORT = 3
MR = 128


NORM_EPS = 1e-06


def doc_starts(doc_lengths, positions):
    doc_ends = jnp.cumsum(doc_lengths)
    doc_firsts = doc_ends - doc_lengths
    before_row = doc_firsts[:, None] <= positions[None, :]
    return jnp.max(jnp.where(before_row, doc_firsts[:, None], 0), axis=0)


def short_conv(raw_rows, prior_rows, tap_rows, positions, starts):
    row_count = raw_rows.shape[1]
    extended = jnp.concatenate([prior_rows, raw_rows], axis=1).astype(jnp.float32)
    running = jnp.zeros(raw_rows.shape, jnp.float32)
    for tap_lag in range(SHORT):
        lagged = lax.slice_in_dim(
            extended, SHORT - 1 - tap_lag, SHORT - 1 - tap_lag + row_count, axis=1
        )
        in_document = positions - tap_lag >= starts
        running = running + jnp.where(
            in_document[None, :], tap_rows[tap_lag][:, None] * lagged, 0.0
        )
    return running


def features(raw_list, prior_list, short_taps, positions, starts):
    gate_conv = short_conv(raw_list[0], prior_list[0], short_taps[0], positions, starts)
    key_conv = short_conv(raw_list[1], prior_list[1], short_taps[1], positions, starts)
    value_conv = short_conv(raw_list[2], prior_list[2], short_taps[2], positions, starts)
    return (gate_conv, (key_conv * value_conv).astype(jnp.bfloat16))


def toeplitz(taps_bf):
    groups = taps_bf.shape[0]
    padded = jnp.concatenate(
        [jnp.zeros((groups, MR), jnp.bfloat16), taps_bf, jnp.zeros((groups, MR + 1), jnp.bfloat16)],
        axis=1,
    )
    repeated = jnp.tile(padded, (1, 2 * MR))[:, : 2 * MR * 3 * MR].reshape(groups, 2 * MR, 3 * MR)
    return repeated[:, :, 2 * MR :]


def long_conv(values, prior_rows, taps_bf, starts):
    channels, row_count = values.shape
    groups = taps_bf.shape[0]
    members = channels // groups
    tile_count = row_count // MR
    blocked = jnp.concatenate([prior_rows, values], axis=1).reshape(channels, tile_count + 1, MR)
    windows = jnp.concatenate([blocked[:, :-1], blocked[:, 1:]], axis=2).reshape(
        groups, members, tile_count, 2 * MR
    )
    matrices = toeplitz(taps_bf)
    per_step = math.gcd(tile_count, max(1, 64 // groups))
    tile_starts = starts.reshape(tile_count, MR)
    source_offsets = jnp.arange(2 * MR, dtype=jnp.int32) - MR
    step_offsets = jnp.arange(per_step, dtype=jnp.int32) * MR
    zero_bf = jnp.zeros((), jnp.bfloat16)

    def advance(step_index, result):
        block_begin = step_index * per_step
        window_part = lax.dynamic_slice_in_dim(windows, block_begin, per_step, axis=2)
        row_starts = lax.dynamic_slice_in_dim(tile_starts, block_begin, per_step, axis=0)
        tile_first = block_begin * MR + step_offsets
        sources = tile_first[:, None] + source_offsets[None, :]
        allowed = sources[:, :, None] >= row_starts[:, None, :]
        masked = jnp.where(allowed[:, None], matrices[None], zero_bf)
        product = jnp.einsum(
            "gcns,ngst->gcnt", window_part, masked, preferred_element_type=jnp.float32
        )
        return lax.dynamic_update_slice_in_dim(result, product, block_begin, axis=2)

    result = lax.fori_loop(
        0,
        tile_count // per_step,
        advance,
        jnp.zeros((groups, members, tile_count, MR), jnp.float32),
    )
    return result.reshape(channels, row_count)


def row_total(partial_value):
    return lax.psum(partial_value, "ch")


def local(
    gate_input, key_input, value_input, short_filter, mr_filter, mr_skip, norm_gain, doc_lengths
):
    ctx_place = lax.axis_index("ctx")
    stacked = jnp.stack([gate_input, key_input, value_input])
    received = lax.all_to_all(stacked, "ctx", split_axis=1, concat_axis=2, tiled=True)
    narrow = received.shape[1]
    all_rows = received.shape[2]
    chan_offset = ctx_place * narrow
    positions = jnp.arange(all_rows, dtype=jnp.int32)
    starts = doc_starts(doc_lengths, positions)
    short_taps = lax.dynamic_slice_in_dim(short_filter, chan_offset, narrow, axis=2)
    zero_prior = jnp.zeros((narrow, SHORT - 1), jnp.bfloat16)
    gate_conv, product_rows = features(
        [received[0], received[1], received[2]],
        [zero_prior, zero_prior, zero_prior],
        short_taps,
        positions,
        starts,
    )
    group_rows = lax.dynamic_slice_in_dim(
        mr_filter, chan_offset // GROUP, max(1, narrow // GROUP), axis=0
    )
    skip_here = lax.dynamic_slice_in_dim(mr_skip, chan_offset, narrow)
    gain_here = lax.dynamic_slice_in_dim(norm_gain, chan_offset, narrow)
    zero_rows = jnp.zeros((narrow, MR), jnp.bfloat16)
    mixed_rows = long_conv(
        product_rows, zero_rows, group_rows.astype(jnp.bfloat16), starts
    ) + skip_here[:, None] * product_rows.astype(jnp.float32)
    gated = gate_conv * mixed_rows
    shares = lax.psum_scatter(
        jnp.sum(gated * gated, axis=0).astype(jnp.bfloat16), "ctx", scatter_dimension=0, tiled=True
    ).astype(jnp.float32)
    own_scale = lax.rsqrt(row_total(shares) / D + NORM_EPS)
    row_scale = lax.all_gather(own_scale, "ctx", axis=0, tiled=True)
    return (gated * row_scale[None, :] * gain_here[:, None]).astype(jnp.bfloat16)


def solution(mesh):
    in_specs = (
        P("ch", "ctx"),
        P("ch", "ctx"),
        P("ch", "ctx"),
        P(None, None, "ch"),
        P("ch", None),
        P("ch"),
        P("ch"),
        P(),
    )
    out_specs = P(("ch", "ctx"), None)
    return jax.shard_map(local, mesh=mesh, in_specs=in_specs, out_specs=out_specs, check_vma=False)
```

profile of v0, /device:TPU:0, one launch (start us, length us, event | category | flops | bytes accessed | tf_op | source)
XLA Modules:
  0.0 258.3 jit_solution(17749262567210162929)
XLA Ops:
  0.0 3.7 %pad_maximum_fusion = bf16[3,2048,512]{2,1,0:T(8,128)(2,1)S(1)} fusion(bf16[1,2048,512]{2,1,0:T(8,128)(2,1)} %bitcast.44, bf16[1,2048,512]{2,1,0:T(8,128)(2,1)} %bitcast.45, bf16[1,2048,512]{2,1,0:T(8,128)(2,1)} %bitcast.46), kind=kLoop, calls=%fused_computation.17 | loop fusion | flops 6291456 | bytes 12582912 | tf_op jit(solution)/shard_map/stack | solution.py:102
  3.7 27.4 %copy.41 = bf16[3,2048,512]{2,0,1:T(4,128)(2,1)} copy(bf16[3,2048,512]{2,1,0:T(8,128)(2,1)S(1)} %pad_maximum_fusion) | data formatting | bytes 12582912 | tf_op jit(solution)/shard_map/stack | solution.py:102
  31.1 5.3 %all-to-all-start = ((bf16[3,2048,512]{2,0,1:T(4,128)(2,1)}), bf16[3,2048,512]{2,0,1:T(4,128)(2,1)}, u32[]{:S(2)}, u32[]{:S(2)}) async-start(bf16[3,2048,512]{2,0,1:T(4,128)(2,1)} %copy.41), calls=%async_computation | async-start | bytes 16777216 | tf_op jit(solution)/shard_map/all_to_all | solution.py:103
  36.7 2.3 tile.4
  39.0 6.6 %tile.10 = bf16[16,98560]{1,0:T(8,128)(2,1)S(1)} reshape(bf16[16,256,385]{2,1,0:T(8,128)(2,1)} %tile.4) | data formatting | bytes 6307840 | tf_op jit(solution)/shard_map/tile | solution.py:52
  45.6 0.2 slice.128
  45.8 0.5 copy.52
  46.4 0.2 slice.129
  46.6 0.8 dynamic_slice.34
  47.3 0.8 dynamic_slice.35
  48.1 0.6 dynamic-slice
  49.3 0.9 constant_dynamic-slice_fusion.5
  50.4 80.6 %all-to-all-done = bf16[3,2048,512]{2,0,1:T(4,128)(2,1)} async-done(((bf16[3,2048,512]{2,0,1:T(4,128)(2,1)}), bf16[3,2048,512]{2,0,1:T(4,128)(2,1)}, u32[]{:S(2)}, u32[]{:S(2)}) %all-to-all-start) | async-done | bytes 6291488 | tf_op jit(solution)/shard_map/all_to_all | solution.py:103
  131.0 13.0 %copy.42 = bf16[3,8,256,512]{2,3,1,0:T(8,128)(2,1)} copy(bf16[3,8,256,512]{3,0,2,1:T(4,128)(2,1)} %bitcast.5) | data formatting | bytes 12582912 | tf_op jit(solution)/shard_map/all_to_all | solution.py:103
  144.0 4.6 %fusion.33 = (bf16[1,256,8,512]{1,3,2,0:T(8,128)(2,1)}, bf16[1,256,8,512]{1,3,2,0:T(8,128)(2,1)S(1)}, bf16[1,256,8,512]{1,3,2,0:T(8,128)(2,1)S(1)}) fusion(bf16[3,256,8,512]{1,3,2,0:T(8,128)(2,1)} %bitcast.35), kind=kLoop, calls=%fused_computation.66 | loop fusion | bytes 12582912 | tf_op jit(solution)/shard_map/slice | solution.py:112
  148.7 0.8 pad_convert_fusion
  149.5 5.1 %fusion.17 = bf16[256,4096]{0,1:T(8,128)(2,1)S(1)} fusion(f32[256,4098]{0,1:T(8,128)S(1)} %get-tuple-element.249, f32[256,4098]{0,1:T(8,128)S(1)} %get-tuple-element.250, f32[256]{0:T(256)S(1)} %bitcast.58, f32[256]{0:T(256)S(1)} %bitcast.53, f32[256]{0:T(256)S(1)} %bitcast.54, f32[256]{0:T(256)S(1)} %bitcast.55, f32[256]{0:T(256)S(1)} %bitcast.56, ...), kind=kLoop, calls=%fused_computation.23 | loop fusion | flops 18874368 | bytes 27281408 | tf_op jit(solution)/shard_map/convert_element_type | solution.py:43
  154.8 0.5 fusion.34
  155.3 2.4 pad_maximum_fusion.1
  157.7 8.0 %copy.43 = bf16[256,32,256]{2,1,0:T(8,128)(2,1)} copy(bf16[256,32,256]{0,2,1:T(8,128)(2,1)} %pad_maximum_fusion.1) | data formatting | bytes 8388608 | tf_op jit(solution)/shard_map/concatenate | solution.py:62
  165.7 2.5 broadcast_in_dim.159.clone
  168.2 28.9 %while.16 = (s32[]{:T(128)}, f32[16,16,32,128]{3,2,1,0:T(8,128)}, s32[32,128]{1,0:T(8,128)S(1)}, bf16[16,256,128]{2,1,0:T(8,128)(2,1)S(1)}, bf16[16,16,32,256]{3...) while((s32[]{:T(128)}, f32[16,16,32,128]{3,2,1,0:T(8,128)}, ...), condition=%wide.region_3.4_spmd.clone, body=%wide.region_2.3_spmd.clone.sunk | while | flops 69338384 | bytes 4473039 | solution.py:85
  168.3 0.2 broadcast_compare_fusion.2
  168.5 1.5 constant_dynamic-slice_fusion.10
  170.0 0.7 fusion.40
  170.7 1.1 copy_dynamic-update-slice_fusion.2
  171.9 0.2 broadcast_compare_fusion.2
  172.1 1.5 constant_dynamic-slice_fusion.10
  173.7 0.7 fusion.40
  174.3 1.1 copy_dynamic-update-slice_fusion.2
  175.5 0.2 broadcast_compare_fusion.2
  175.7 1.5 constant_dynamic-slice_fusion.10
  177.3 0.7 fusion.40
  178.0 1.1 copy_dynamic-update-slice_fusion.2
  179.1 0.2 broadcast_compare_fusion.2
  179.3 1.5 constant_dynamic-slice_fusion.10
  180.9 0.7 fusion.40
  181.6 1.1 copy_dynamic-update-slice_fusion.2
  182.8 0.2 broadcast_compare_fusion.2
  183.0 1.5 constant_dynamic-slice_fusion.10
  184.5 0.7 fusion.40
  185.2 1.0 copy_dynamic-update-slice_fusion.2
  186.3 0.2 broadcast_compare_fusion.2
  186.6 1.5 constant_dynamic-slice_fusion.10
  188.1 0.7 fusion.40
  188.8 1.1 copy_dynamic-update-slice_fusion.2
  190.0 0.2 broadcast_compare_fusion.2
  190.2 1.5 constant_dynamic-slice_fusion.10
  191.7 0.7 fusion.40
  192.4 1.1 copy_dynamic-update-slice_fusion.2
  193.6 0.2 broadcast_compare_fusion.2
  193.8 1.5 constant_dynamic-slice_fusion.10
  195.3 0.7 fusion.40
  196.0 1.1 copy_dynamic-update-slice_fusion.2
  197.1 7.9 %copy.58 = f32[32,8,32,128]{3,1,2,0:T(8,128)} copy(f32[32,8,32,128]{3,2,1,0:T(8,128)} %bitcast.28) | data formatting | bytes 8388608
  205.0 5.6 %copy.46 = f32[256,4096]{0,1:T(8,128)} copy(f32[256,4096]{1,0:T(8,128)} %bitcast.37) | data formatting | bytes 8388608 | tf_op jit(solution)/shard_map/reshape | solution.py:91
  210.6 2.1 pad_convert_fusion.2
  212.7 0.7 copy-done.2
  213.4 5.7 %multiply_reduce_fusion = (bf16[4096]{0:T(1024)(128)(2,1)S(1)}, f32[256,4096]{0,1:T(8,128)}) fusion(f32[256,4096]{0,1:T(8,128)S(1)} %copy-done.2, bf16[256,4096]{0,1:T(8,128)(2,1)S(1)} %fusion.17, f32[256]{0:T(256)S(1)} %dynamic_slice.34, f32[256,4098]{0,1:T(8,128)S(1)} %pad_convert_fusion.2, f32[256]{0:T(256)S(1)} %bitcast.51, ...), kind=kLoop, calls=%fused_computation.48 | loop fusion | flops 14675968 | bytes 23093248 | tf_op jit(solution)/shard_map/reduce_sum | solution.py:129
  219.1 12.1 %all-reduce.4 = bf16[4096]{0:T(1024)(128)(2,1)S(1)} all-reduce(bf16[4096]{0:T(1024)(128)(2,1)S(1)} %get-tuple-element.230), channel_id=2, replica_groups=mesh['ctx'=8,'ch'=4] {'ctx'}, use_global_device_ids=true, to_apply=%region_5.6.clone | all-reduce | flops 4096 | bytes 16384
  231.4 12.6 %psum.7 = f32[512]{0:T(512)S(1)} all-reduce(f32[512]{0:T(512)S(1)} %dynamic-slice_convert_fusion.1), channel_id=1, replica_groups=mesh['ctx'=8,'ch'=4] {'ch'}, use_global_device_ids=true, to_apply=%region_6.7 | all-reduce | flops 512 | bytes 4096 | tf_op jit(solution)/shard_map/psum | solution.py:95
  244.0 8.9 %all-gather = f32[8,1,512]{2,1,0:T(1,128)S(1)} all-gather(f32[1,1,512]{2,1,0:T(1,128)S(1)} %bitcast.49), channel_id=1, replica_groups=mesh['ctx'=8,'ch'=4] {'ctx'}, dimensions={0}, use_global_device_ids=true | all-gather | bytes 18432 | tf_op jit(solution)/shard_map/all_gather | solution.py:132
  252.8 2.6 %multiply_convert_fusion = bf16[256,4096]{0,1:T(8,128)(2,1)S(1)} fusion(f32[256,4096]{0,1:T(8,128)} %get-tuple-element.231, f32[256]{0:T(256)S(1)} %dynamic_slice.35, f32[4096]{0:T(1024)S(1)} %bitcast.48), kind=kLoop, calls=%fused_computation.47 | loop fusion | flops 3145728 | bytes 6308864 | tf_op jit(solution)/shard_map/convert_element_type | solution.py:133
  255.5 2.9 %copy.47 = bf16[256,4096]{1,0:T(8,128)(2,1)} copy(bf16[256,4096]{0,1:T(8,128)(2,1)S(1)} %multiply_convert_fusion) | data formatting | bytes 4194304 | tf_op jit(solution)/shard_map/convert_element_type | solution.py:133
  (56 shorter events, 1.4 us)
Async XLA Ops:
  0.0 36.7 %copy-start = (f32[128,128]{1,0:T(8,128)S(1)}, f32[128,128]{1,0:T(8,128)}, u32[]{:S(2)}) copy-start(f32[128,128]{1,0:T(8,128)} %param.14) | copy-start | bytes 196612
  31.1 5.3 %copy-start.3 = (s32[16]{0:T(128)S(1)}, s32[16]{0:T(128)}, u32[]{:S(2)}) copy-start(s32[16]{0:T(128)} %param.17) | copy-start | bytes 196
  31.1 100.0 %all-to-all-start = ((bf16[3,2048,512]{2,0,1:T(4,128)(2,1)}), bf16[3,2048,512]{2,0,1:T(4,128)(2,1)}, u32[]{:S(2)}, u32[]{:S(2)}) async-start(bf16[3,2048,512]{2,0,1:T(4,128)(2,1)} %copy.41), calls=%async_computation | async-start | bytes 16777216 | tf_op jit(solution)/shard_map/all_to_all | solution.py:103
  45.8 2.3 copy-start.4
  210.6 2.8 %copy-start.2 = (f32[256,4096]{0,1:T(8,128)S(1)}, f32[256,4096]{0,1:T(8,128)}, u32[]{:S(2)}) copy-start(f32[256,4096]{0,1:T(8,128)} %copy.46) | copy-start | bytes 12582916
  252.8 5.5 %copy-start.1 = (f32[128,128]{1,0:T(8,128)S(1)}, f32[128,128]{1,0:T(8,128)}, u32[]{:S(2)}) copy-start(f32[128,128]{1,0:T(8,128)} %param.14) | copy-start | bytes 196612
where the time goes:
time: 260 us; the launch traced here: 258 us
  local copies, waits for them, and re-layouts  107 us (41%)
  waiting for transfers between devices  80.6 us (31%)
  blocking collectives  33.6 us (13%)
  other arithmetic  25.2 us (10%)
  matrix products  5.4 us (2%)
  starting transfers between devices  5.3 us (2%)
    all_to_all x1, waiting for transfers between devices, local(): lax.all_to_all(stacked, 'ctx', split_axis=1, concat_axis=2, tiled=True)  80.6 us
    another operation x1, local copies, waits for them, and re-layouts, local(): stacked = jnp.stack([gate_input, key_input, value_input])  27.4 us
    all_to_all x1, local copies, waits for them, and re-layouts, local(): lax.all_to_all(stacked, 'ctx', split_axis=1, concat_axis=2, tiled=True)  13 us
    psum x1, blocking collectives, row_total(): return lax.psum(partial_value, 'ch')  12.6 us
    dynamic_slice x8, local copies, waits for them, and re-layouts, advance(): lax.dynamic_slice_in_dim(windows, block_begin, per_step, axis=2)  12.3 us
    unnamed x1, blocking collectives  12.1 us
    unnamed x13, local copies, waits for them, and re-layouts  9.7 us
    all_gather x1, blocking collectives, local(): row_scale = lax.all_gather(own_scale, 'ctx', axis=0, tiled=True)  8.88 us
  transfers between devices with their start and end apart: 1, of which 1 were waited for; matrix products, arithmetic and copies ran while one was open for 5% of the time, Pallas kernels for 0%

commit v1 on v0

v1 whole, which is shorter than its diff:
```python
import functools

import jax
import jax.numpy as jnp
from jax import lax
from jax.experimental import pallas as pl
from jax.experimental.pallas import tpu as pltpu
from jax.sharding import PartitionSpec as P

D = 8192
GROUP = 16
SHORT = 3
MR = 128
NORM_EPS = 1e-06

LANES = 128
BLOCK = 256
F32 = jnp.float32
BF16 = jnp.bfloat16


def short_conv(ext_ref, coef_ref, rows, first_tile, tiles, which, m1, m2):
    width = (tiles + 1) * LANES
    x = ext_ref[rows, first_tile * LANES : first_tile * LANES + width].astype(F32)
    x1 = pltpu.roll(x, 1, 1)[:, LANES:]
    x2 = pltpu.roll(x, 2, 1)[:, LANES:]
    base = which * SHORT
    c0 = coef_ref[rows, base : base + 1]
    c1 = coef_ref[rows, base + 1 : base + 2]
    c2 = coef_ref[rows, base + 2 : base + 3]
    return c0 * x[:, LANES:] + c1 * (x1 * m1) + c2 * (x2 * m2)


def kernel(
    n,
    nz,
    gate_hbm,
    key_hbm,
    value_hbm,
    sf_ref,
    mr_ref,
    skip_ref,
    docs_ref,
    recv_ref,
    scale_ref,
    g_ext,
    k_ext,
    v_ext,
    p_ext,
    circ,
    coef,
    masks,
    lagmask,
    sendbuf,
    raw_send,
    raw_recv,
    acc,
    sq_all,
    sc_all,
    load_sem,
    halo_send,
    halo_recv,
    data_send,
    data_recv,
    sq_send,
    sq_recv,
    sc_send,
    sc_recv,
):
    me = lax.axis_index("ctx")
    mz = lax.axis_index("ch")
    channels, rows_here = gate_hbm.shape
    chunk = channels // n
    groups = channels // GROUP
    tiles = rows_here // LANES
    blocks = channels // BLOCK
    barrier = pltpu.get_barrier_semaphore()

    def load(b, which):
        source = (gate_hbm, key_hbm, value_hbm)[which]
        target = (g_ext, k_ext, v_ext)[which]
        span = pl.ds(pl.multiple_of(b * BLOCK, BLOCK), BLOCK)
        return pltpu.make_async_copy(
            source.at[span, :],
            target.at[span, LANES : LANES + rows_here],
            load_sem.at[b, which],
        )

    for b in range(blocks):
        for which in range(3):
            load(b, which).start()
    for k in range(1, n):
        pl.semaphore_signal(barrier, inc=1, device_id={"ctx": lax.rem(me + k, n)})
    for k in range(1, nz):
        pl.semaphore_signal(barrier, inc=1, device_id={"ch": lax.rem(mz + k, nz)})

    positions = me * rows_here + lax.broadcasted_iota(jnp.int32, (1, rows_here), 1)
    starts = jnp.zeros((1, rows_here), jnp.int32)
    first = jnp.int32(0)
    for d in range(docs_ref.shape[0]):
        starts = jnp.where(positions >= first, first, starts)
        first = first + docs_ref[d]
    for lag in (1, 2):
        lagmask[lag : lag + 1, :] = jnp.where(positions - lag >= starts, 1.0, 0.0).astype(F32)
    s_index = lax.broadcasted_iota(jnp.int32, (LANES, LANES), 0)
    t_index = lax.broadcasted_iota(jnp.int32, (LANES, LANES), 1)
    for tile in range(tiles):
        start_row = starts[:, tile * LANES : (tile + 1) * LANES]
        here = me * rows_here + tile * LANES + s_index
        before = (t_index < s_index) & (here - LANES >= start_row)
        within = (t_index >= s_index) & (here >= start_row)
        masks[tile, 0:LANES, :] = jnp.where(before, 1.0, 0.0).astype(BF16)
        masks[tile, LANES : 2 * LANES, :] = jnp.where(within, 1.0, 0.0).astype(BF16)

    for b in range(channels // LANES):
        span = slice(b * LANES, (b + 1) * LANES)
        parts = [sf_ref[a, :, span] for a in range(3)] + [skip_ref[:, span]]
        parts.append(jnp.zeros((LANES - 10, LANES), F32))
        coef[span, :] = jnp.concatenate(parts, axis=0).T

    row16 = lax.broadcasted_iota(jnp.int32, (16, LANES), 0)
    lane16 = lax.broadcasted_iota(jnp.int32, (16, LANES), 1)

    def pick(which):
        hit = (lane16 - (LANES - 2) == row16 - 2 * which) & (lane16 >= LANES - 2)
        return jnp.where(hit, 1.0, 0.0).astype(BF16)

    last = tiles * LANES

    def halo_block(b, carry):
        for which in range(3):
            load(b, which).wait()
        span = pl.ds(pl.multiple_of(b * BLOCK, BLOCK), BLOCK)
        columns = jnp.zeros((16, BLOCK), F32)
        for which, ref in enumerate((g_ext, k_ext, v_ext)):
            columns = columns + lax.dot_general(
                pick(which),
                ref[span, last : last + LANES],
                (((1,), (1,)), ((), ())),
                preferred_element_type=F32,
            )
        raw_send[:, span] = columns.astype(BF16)
        m1 = lagmask[1:2, last - LANES : last]
        m2 = lagmask[2:3, last - LANES : last]

        def halo_rows(i, c):
            rows = pl.ds(pl.multiple_of(b * BLOCK + i * 32, 32), 32)
            kc = short_conv(k_ext, coef, rows, tiles - 1, 1, 1, m1, m2)
            vc = short_conv(v_ext, coef, rows, tiles - 1, 1, 2, m1, m2)
            p_ext[rows, last : last + LANES] = (kc * vc).astype(BF16)
            return c

        lax.fori_loop(0, BLOCK // 32, halo_rows, 0, unroll=2)
        return carry

    lax.fori_loop(0, blocks, halo_block, 0)

    pl.semaphore_wait(barrier, n - 1 + nz - 1)
    right = lax.rem(me + 1, n)

    def raw_copy():
        return pltpu.make_async_remote_copy(
            src_ref=raw_send,
            dst_ref=raw_recv,
            send_sem=halo_send.at[0],
            recv_sem=halo_recv.at[0],
            device_id={"ctx": right},
        )

    def product_copy():
        return pltpu.make_async_remote_copy(
            src_ref=p_ext.at[:, last : last + LANES],
            dst_ref=p_ext.at[:, 0:LANES],
            send_sem=halo_send.at[1],
            recv_sem=halo_recv.at[1],
            device_id={"ctx": right},
        )

    @pl.when(me < n - 1)
    def _():
        raw_copy().start()
        product_copy().start()

    @pl.when(me == 0)
    def _():
        raw_recv[...] = jnp.zeros(raw_recv.shape, BF16)
        p_ext[:, 0:LANES] = jnp.zeros((channels, LANES), BF16)

    def build(g, carry):
        taps = jnp.broadcast_to(mr_ref[pl.ds(g, 1), :], (LANES, LANES))
        turned = pltpu.roll(taps, 0, 1, stride=1, stride_axis=0)
        circ[g] = turned.astype(BF16)
        return carry

    lax.fori_loop(0, groups, build, 0, unroll=2)

    @pl.when(me > 0)
    def _():
        raw_copy().wait_recv()

    def spread(b, carry):
        span = pl.ds(pl.multiple_of(b * BLOCK, BLOCK), BLOCK)
        for which, ref in enumerate((g_ext, k_ext, v_ext)):
            ref[span, 0:LANES] = lax.dot_general(
                raw_recv[:, span],
                pick(which),
                (((0,), (0,)), ((), ())),
                preferred_element_type=F32,
            ).astype(BF16)
        return carry

    lax.fori_loop(0, blocks, spread, 0)

    def products(i, carry):
        rows = pl.ds(pl.multiple_of(i * GROUP, GROUP), GROUP)
        m1 = lagmask[1:2, 0 : last - LANES]
        m2 = lagmask[2:3, 0 : last - LANES]
        kc = short_conv(k_ext, coef, rows, 0, tiles - 1, 1, m1, m2)
        vc = short_conv(v_ext, coef, rows, 0, tiles - 1, 2, m1, m2)
        p_ext[rows, LANES:last] = (kc * vc).astype(BF16)
        return carry

    lax.fori_loop(0, groups, products, 0, unroll=2)

    acc[...] = jnp.zeros(acc.shape, F32)

    def mix(g, first_tile, count):
        rows = pl.ds(pl.multiple_of(g * GROUP, GROUP), GROUP)
        lanes = slice(first_tile * LANES, (first_tile + count) * LANES)
        c = circ[g]
        pair = jnp.concatenate([c, c], axis=0)
        parts = []
        for tile in range(first_tile, first_tile + count):
            parts.append(
                jnp.dot(
                    p_ext[rows, tile * LANES : (tile + 2) * LANES],
                    pair * masks[tile],
                    preferred_element_type=F32,
                )
            )
        mixed = parts[0] if count == 1 else jnp.concatenate(parts, axis=1)
        direct = p_ext[rows, (first_tile + 1) * LANES : (first_tile + 1 + count) * LANES]
        mixed = mixed + coef[rows, 9:10] * direct.astype(F32)
        gate = short_conv(
            g_ext, coef, rows, first_tile, count, 0, lagmask[1:2, lanes], lagmask[2:3, lanes]
        )
        gated = gate * mixed
        sendbuf[rows, lanes] = gated.astype(BF16)
        squares = gated * gated
        return squares[0:8] + squares[8:16]

    def data_copy(dest, source, half):
        lanes = (LANES, last - LANES) if half == 0 else (0, LANES)
        return pltpu.make_async_remote_copy(
            src_ref=sendbuf.at[
                pl.ds(pl.multiple_of(dest * chunk, chunk), chunk), lanes[0] : lanes[0] + lanes[1]
            ],
            dst_ref=recv_ref.at[
                :, pl.ds(pl.multiple_of(source * rows_here + lanes[0], LANES), lanes[1])
            ],
            send_sem=data_send.at[dest, half],
            recv_sem=data_recv.at[source, half],
            device_id={"ctx": dest},
        )

    def own_copy(half):
        lanes = (LANES, last - LANES) if half == 0 else (0, LANES)
        return pltpu.make_async_copy(
            sendbuf.at[
                pl.ds(pl.multiple_of(me * chunk, chunk), chunk), lanes[0] : lanes[0] + lanes[1]
            ],
            recv_ref.at[:, pl.ds(pl.multiple_of(me * rows_here + lanes[0], LANES), lanes[1])],
            data_send.at[me, half],
        )

    def stage(half, first_tile, count, together):
        lanes = slice(first_tile * LANES, (first_tile + count) * LANES)
        chunk_groups = chunk // GROUP

        def one(step, carry):
            k = lax.rem(step + 2, n)
            dest = lax.rem(me + k, n)

            def some(i, c):
                total = jnp.zeros((8, count * LANES), F32)
                for j in range(together):
                    total = total + mix(
                        dest * chunk_groups + i * together + j, first_tile, count
                    )
                acc[:, lanes] += total
                return c

            lax.fori_loop(0, chunk_groups // together, some, 0)

            @pl.when(k != 0)
            def _():
                data_copy(dest, me, half).start()

            @pl.when(k == 0)
            def _():
                own_copy(half).start()

            return carry

        lax.fori_loop(0, n, one, 0)

    stage(0, 1, tiles - 1, 2)

    @pl.when(me > 0)
    def _():
        product_copy().wait_recv()

    stage(1, 0, 1, 2)

    sq_all[mz] = jnp.sum(acc[...], axis=0, keepdims=True)

    def sq_copy(dest, source):
        return pltpu.make_async_remote_copy(
            src_ref=sq_all.at[mz],
            dst_ref=sq_all.at[source],
            send_sem=sq_send.at[dest],
            recv_sem=sq_recv.at[source],
            device_id={"ch": dest},
        )

    for k in range(1, nz):
        sq_copy(lax.rem(mz + k, nz), mz).start()
    for k in range(1, nz):
        sq_copy(mz, lax.rem(mz + k, nz)).wait_recv()
    total = sq_all[0]
    for z in range(1, nz):
        total = total + sq_all[z]
    sc_all[me] = lax.rsqrt(total / D + NORM_EPS)

    def sc_copy(dest, source):
        return pltpu.make_async_remote_copy(
            src_ref=sc_all.at[me],
            dst_ref=sc_all.at[source],
            send_sem=sc_send.at[dest],
            recv_sem=sc_recv.at[source],
            device_id={"ctx": dest},
        )

    for k in range(1, n):
        sc_copy(lax.rem(me + k, n), me).start()
    for k in range(1, n):
        sc_copy(me, lax.rem(me + k, n)).wait_recv()
    scale_ref[...] = sc_all[...]

    def finish(k, carry):
        other = lax.rem(me + k, n)
        for half in (0, 1):
            data_copy(me, other, half).wait_recv()
            data_copy(other, me, half).wait_send()
        sc_copy(other, me).wait_send()
        return carry

    lax.fori_loop(1, n, finish, 0)
    own_copy(0).wait()
    own_copy(1).wait()
    for k in range(1, nz):
        sq_copy(lax.rem(mz + k, nz), mz).wait_send()

    @pl.when(me < n - 1)
    def _():
        raw_copy().wait_send()
        product_copy().wait_send()


def local(
    n, nz, gate_input, key_input, value_input, short_filter, mr_filter, mr_skip, norm_gain, doc_lengths
):
    channels, rows_here = gate_input.shape
    chunk = channels // n
    groups = channels // GROUP
    tiles = rows_here // LANES
    ext = pltpu.VMEM((channels, rows_here + LANES), BF16)
    anywhere = pl.BlockSpec(memory_space=pl.ANY)
    vmem = pl.BlockSpec(memory_space=pltpu.VMEM)
    dma = pltpu.SemaphoreType.DMA
    received, scales = pl.pallas_call(
        functools.partial(kernel, n, nz),
        out_shape=(
            jax.ShapeDtypeStruct((chunk, n * rows_here), BF16),
            jax.ShapeDtypeStruct((n, 1, rows_here), F32),
        ),
        in_specs=[
            anywhere,
            anywhere,
            anywhere,
            vmem,
            vmem,
            vmem,
            pl.BlockSpec(memory_space=pltpu.SMEM),
        ],
        out_specs=(anywhere, vmem),
        scratch_shapes=[
            ext,
            ext,
            ext,
            ext,
            pltpu.VMEM((groups, LANES, LANES), BF16),
            pltpu.VMEM((channels, LANES), F32),
            pltpu.VMEM((tiles, 2 * LANES, LANES), BF16),
            pltpu.VMEM((8, rows_here), F32),
            pltpu.VMEM((channels, rows_here), BF16),
            pltpu.VMEM((16, channels), BF16),
            pltpu.VMEM((16, channels), BF16),
            pltpu.VMEM((8, rows_here), F32),
            pltpu.VMEM((nz, 1, rows_here), F32),
            pltpu.VMEM((n, 1, rows_here), F32),
            dma((channels // BLOCK, 3)),
            dma((2,)),
            dma((2,)),
            dma((n, 2)),
            dma((n, 2)),
            dma((nz,)),
            dma((nz,)),
            dma((n,)),
            dma((n,)),
        ],
        compiler_params=pltpu.CompilerParams(
            collective_id=0, has_side_effects=True, vmem_limit_bytes=40 * 1024 * 1024
        ),
        cost_estimate=pl.CostEstimate(
            flops=channels * rows_here * 600, bytes_accessed=channels * rows_here * 8, transcendentals=0
        ),
    )(
        gate_input,
        key_input,
        value_input,
        short_filter,
        mr_filter,
        mr_skip.reshape(1, channels),
        doc_lengths,
    )
    gain_here = lax.dynamic_slice_in_dim(norm_gain, lax.axis_index("ctx") * chunk, chunk)
    row_scale = scales.reshape(1, n * rows_here)
    return (received.astype(F32) * row_scale * gain_here[:, None]).astype(BF16)


def solution(mesh):
    n, nz = mesh.shape["ctx"], mesh.shape["ch"]
    in_specs = (
        P("ch", "ctx"),
        P("ch", "ctx"),
        P("ch", "ctx"),
        P(None, None, "ch"),
        P("ch", None),
        P("ch"),
        P("ch"),
        P(),
    )
    out_specs = P(("ch", "ctx"), None)
    return jax.shard_map(
        functools.partial(local, n, nz), mesh=mesh, in_specs=in_specs, out_specs=out_specs, check_vma=False
    )
```

time: 260 us -> 69.2 us (0.27)
  local copies, waits for them, and re-layouts: 107 us -> 8.61 us
  waiting for transfers between devices: 80.6 us -> 0 us
  Pallas kernels: 0 us -> 58.3 us
  blocking collectives: 33.6 us -> 0 us
  other arithmetic: 25.2 us -> 1.9 us
  matrix products: 5.4 us -> 0 us
  starting transfers between devices: 5.3 us -> 0 us
    all_to_all x1 -> x0, waiting for transfers between devices: 80.6 us -> none  [local(): lax.all_to_all(stacked, 'ctx', split_axis=1, concat_axis=2, tiled=True)]
    pallas_call x0 -> x1, Pallas kernels: none -> 58.3 us  [local(): pl.pallas_call(functools.partial(kernel, n, nz), out_shape=(jax.ShapeDtyp...]
    another operation x4 -> x0, local copies, waits for them, and re-layouts: 36.3 us -> none  [the longest x1 27.4 us: local(): stacked = jnp.stack([gate_input, key_input, value_input])]
    dynamic_slice x18 -> x1, local copies, waits for them, and re-layouts: 13.9 us -> 0.76 us  [local(): lax.dynamic_slice_in_dim(norm_gain, lax.axis_index('ctx') * chunk, chunk)]
    all_to_all x1 -> x0, local copies, waits for them, and re-layouts: 13 us -> none  [local(): lax.all_to_all(stacked, 'ctx', split_axis=1, concat_axis=2, tiled=True)]
    psum x1 -> x0, blocking collectives: 12.6 us -> none  [row_total(): return lax.psum(partial_value, 'ch')]
    unnamed x1 -> x0, blocking collectives: 12.1 us -> none
    convert_element_type x5 -> x1, other arithmetic: 10.8 us -> 1.9 us  [local(): return (received.astype(F32) * row_scale * gain_here[:, None]).astype(BF16)]
  transfers between devices with their start and end apart: 1 -> 0, of which waited for: 1 -> 0; matrix products, arithmetic and copies ran while one was open for 5% -> 0% of each run, Pallas kernels for 0% -> 0%
where the time goes in v1:
time: 69.2 us; the launch traced here: 68.8 us
  Pallas kernels  58.3 us (84%)
  local copies, waits for them, and re-layouts  8.61 us (12%)
  other arithmetic  1.9 us (3%)
    pallas_call x1, Pallas kernels, local(): pl.pallas_call(functools.partial(kernel, n, nz), out_shape=(jax.ShapeDtyp...  58.3 us
    unnamed x14, local copies, waits for them, and re-layouts  7.85 us
    convert_element_type x1, other arithmetic, local(): return (received.astype(F32) * row_scale * gain_here[:, None]).astype(BF16)  1.9 us

profile of v1, /device:TPU:0, one launch (start us, length us, event | category | flops | bytes accessed | tf_op | source)
XLA Modules:
  0.0 68.8 jit_solution(11596531906224083307)
XLA Ops:
  0.0 0.8 %dynamic_slice.3 = f32[256]{0:T(256)S(1)} dynamic-slice(f32[2048]{0:T(1024)} %param.14, s32[]{:T(128)S(6)} %select_n.3), dynamic_slice_sizes={256} | dynamic-slice | bytes 2052 | tf_op jit(solution)/shard_map/dynamic_slice | solution.py:437
  0.8 0.0 copy-start
  0.8 1.6 %copy-done = bf16[2048,512]{1,0:T(8,128)(2,1)S(1)} copy-done((bf16[2048,512]{1,0:T(8,128)(2,1)S(1)}, bf16[2048,512]{1,0:T(8,128)(2,1)}, u32[]{:S(2)}) %copy-start) | copy-done | bytes 2097176
  2.4 0.0 copy-start.1
  2.4 1.6 %copy-done.1 = bf16[2048,512]{1,0:T(8,128)(2,1)S(1)} copy-done((bf16[2048,512]{1,0:T(8,128)(2,1)S(1)}, bf16[2048,512]{1,0:T(8,128)(2,1)}, u32[]{:S(2)}) %copy-start.1) | copy-done | bytes 2097176
  3.9 0.0 copy-start.2
  3.9 1.6 %copy-done.2 = bf16[2048,512]{1,0:T(8,128)(2,1)S(1)} copy-done((bf16[2048,512]{1,0:T(8,128)(2,1)S(1)}, bf16[2048,512]{1,0:T(8,128)(2,1)}, u32[]{:S(2)}) %copy-start.2) | copy-done | bytes 2097176
  5.5 0.0 copy-start.3
  5.5 0.9 %copy-done.3 = f32[3,3,2048]{2,1,0:T(4,128)S(1)} copy-done((f32[3,3,2048]{2,1,0:T(4,128)S(1)}, f32[3,3,2048]{2,1,0:T(4,128)}, u32[]{:S(2)}) %copy-start.3) | copy-done | bytes 73752
  6.4 0.0 copy-start.4
  6.4 0.8 %copy-done.4 = f32[128,128]{1,0:T(8,128)S(1)} copy-done((f32[128,128]{1,0:T(8,128)S(1)}, f32[128,128]{1,0:T(8,128)}, u32[]{:S(2)}) %copy-start.4) | copy-done | bytes 65560
  7.3 0.0 copy-start.5
  7.3 0.7 %copy-done.5 = f32[2048]{0:T(1024)S(1)} copy-done((f32[2048]{0:T(1024)S(1)}, f32[2048]{0:T(1024)}, u32[]{:S(2)}) %copy-start.5) | copy-done | bytes 8216
  8.0 0.0 copy-start.6
  8.0 0.7 copy-done.6
  8.6 58.3 %shard_map.82 = (bf16[256,4096]{1,0:T(8,128)(2,1)S(1)}, f32[8,1,512]{2,1,0:T(1,128)S(1)}) custom-call(bf16[2048,512]{1,0:T(8,128)(2,1)S(1)} %copy-done, bf16[2048,512]{1,0:T(8,128)(2,1)S(1)} %copy-done.1, bf16[2048,512]{1,0:T(8,128)(2,1)S(1)} %copy-done.2, f32[3,3,2048]{2,1,0:T(4,128)S(1)} %copy-done.3, f32[128,128]{1,0:T(8,128)S(1)} %copy-done.4, ...), custom_call_target="tpu_custom_call" | custom-call | flops 629145600 | bytes 8388608 | tf_op jit(solution)/shard_map/pallas_call | solution.py:381
  66.9 1.9 %multiply_convert_fusion = bf16[256,4096]{1,0:T(8,128)(2,1)} fusion(bf16[256,4096]{1,0:T(8,128)(2,1)S(1)} %get-tuple-element.7, f32[256]{0:T(256)S(1)} %dynamic_slice.3, f32[4096]{0:T(1024)S(1)} %bitcast.2), kind=kLoop, calls=%fused_computation | loop fusion | flops 4194304 | bytes 4211712 | tf_op jit(solution)/shard_map/convert_element_type | solution.py:439
Async XLA Ops:
  0.8 1.6 %copy-start = (bf16[2048,512]{1,0:T(8,128)(2,1)S(1)}, bf16[2048,512]{1,0:T(8,128)(2,1)}, u32[]{:S(2)}) copy-start(bf16[2048,512]{1,0:T(8,128)(2,1)} %gate_hbm.1) | copy-start | bytes 6291460
  2.4 1.6 %copy-start.1 = (bf16[2048,512]{1,0:T(8,128)(2,1)S(1)}, bf16[2048,512]{1,0:T(8,128)(2,1)}, u32[]{:S(2)}) copy-start(bf16[2048,512]{1,0:T(8,128)(2,1)} %key_hbm.1) | copy-start | bytes 6291460
  3.9 1.6 %copy-start.2 = (bf16[2048,512]{1,0:T(8,128)(2,1)S(1)}, bf16[2048,512]{1,0:T(8,128)(2,1)}, u32[]{:S(2)}) copy-start(bf16[2048,512]{1,0:T(8,128)(2,1)} %value_hbm.1) | copy-start | bytes 6291460
  5.5 0.9 %copy-start.3 = (f32[3,3,2048]{2,1,0:T(4,128)S(1)}, f32[3,3,2048]{2,1,0:T(4,128)}, u32[]{:S(2)}) copy-start(f32[3,3,2048]{2,1,0:T(4,128)} %sf_ref.1) | copy-start | bytes 221188
  6.4 0.8 %copy-start.4 = (f32[128,128]{1,0:T(8,128)S(1)}, f32[128,128]{1,0:T(8,128)}, u32[]{:S(2)}) copy-start(f32[128,128]{1,0:T(8,128)} %mr_ref.1) | copy-start | bytes 196612
  7.3 0.7 %copy-start.5 = (f32[2048]{0:T(1024)S(1)}, f32[2048]{0:T(1024)}, u32[]{:S(2)}) copy-start(f32[2048]{0:T(1024)} %param.13) | copy-start | bytes 24580
  8.0 0.7 copy-start.6

commit v2 on v1

--- a/solution.py
+++ b/solution.py
@@ -37,9 +37,9 @@
     gate_hbm,
     key_hbm,
     value_hbm,
-    sf_ref,
-    mr_ref,
-    skip_ref,
+    sf_hbm,
+    mr_hbm,
+    skip_hbm,
     docs_ref,
     recv_ref,
     scale_ref,
@@ -57,6 +57,10 @@
     acc,
     sq_all,
     sc_all,
+    sf_ref,
+    mr_ref,
+    skip_ref,
+    small_sem,
     load_sem,
     halo_send,
     halo_recv,
@@ -86,6 +90,14 @@
             load_sem.at[b, which],
         )
 
+    small = [
+        pltpu.make_async_copy(source, target, small_sem.at[i])
+        for i, (source, target) in enumerate(
+            ((sf_hbm, sf_ref), (skip_hbm, skip_ref), (mr_hbm, mr_ref))
+        )
+    ]
+    for copy in small:
+        copy.start()
     for b in range(blocks):
         for which in range(3):
             load(b, which).start()
@@ -112,11 +124,14 @@
         masks[tile, 0:LANES, :] = jnp.where(before, 1.0, 0.0).astype(BF16)
         masks[tile, LANES : 2 * LANES, :] = jnp.where(within, 1.0, 0.0).astype(BF16)
 
+    for copy in small:
+        copy.wait()
+
     for b in range(channels // LANES):
         span = slice(b * LANES, (b + 1) * LANES)
         parts = [sf_ref[a, :, span] for a in range(3)] + [skip_ref[:, span]]
-        parts.append(jnp.zeros((LANES - 10, LANES), F32))
-        coef[span, :] = jnp.concatenate(parts, axis=0).T
+        parts.append(jnp.zeros((6, LANES), F32))
+        coef[span, 0:16] = jnp.concatenate(parts, axis=0).T
 
     row16 = lax.broadcasted_iota(jnp.int32, (16, LANES), 0)
     lane16 = lax.broadcasted_iota(jnp.int32, (16, LANES), 1)
@@ -150,7 +165,7 @@
             p_ext[rows, last : last + LANES] = (kc * vc).astype(BF16)
             return c
 
-        lax.fori_loop(0, BLOCK // 32, halo_rows, 0, unroll=2)
+        lax.fori_loop(0, BLOCK // 32, halo_rows, 0, unroll=4)
         return carry
 
     lax.fori_loop(0, blocks, halo_block, 0)
@@ -191,8 +206,6 @@
         turned = pltpu.roll(taps, 0, 1, stride=1, stride_axis=0)
         circ[g] = turned.astype(BF16)
         return carry
-
-    lax.fori_loop(0, groups, build, 0, unroll=2)
 
     @pl.when(me > 0)
     def _():
@@ -219,8 +232,6 @@
         vc = short_conv(v_ext, coef, rows, 0, tiles - 1, 2, m1, m2)
         p_ext[rows, LANES:last] = (kc * vc).astype(BF16)
         return carry
-
-    lax.fori_loop(0, groups, products, 0, unroll=2)
 
     acc[...] = jnp.zeros(acc.shape, F32)
 
@@ -281,6 +292,16 @@
             k = lax.rem(step + 2, n)
             dest = lax.rem(me + k, n)
 
+            if half == 0:
+                first = dest * chunk_groups
+                unroll = min(4, chunk_groups)
+                lax.fori_loop(
+                    0, chunk_groups, lambda i, c: build(first + i, c), 0, unroll=unroll
+                )
+                lax.fori_loop(
+                    0, chunk_groups, lambda i, c: products(first + i, c), 0, unroll=unroll
+                )
+
             def some(i, c):
                 total = jnp.zeros((8, count * LANES), F32)
                 for j in range(together):
@@ -304,13 +325,14 @@
 
         lax.fori_loop(0, n, one, 0)
 
-    stage(0, 1, tiles - 1, 2)
+    together = min(8, chunk // GROUP)
+    stage(0, 1, tiles - 1, together)
 
     @pl.when(me > 0)
     def _():
         product_copy().wait_recv()
 
-    stage(1, 0, 1, 2)
+    stage(1, 0, 1, together)
 
     sq_all[mz] = jnp.sum(acc[...], axis=0, keepdims=True)
 
@@ -388,9 +410,9 @@
             anywhere,
             anywhere,
             anywhere,
-            vmem,
-            vmem,
-            vmem,
+            anywhere,
+            anywhere,
+            anywhere,
             pl.BlockSpec(memory_space=pltpu.SMEM),
         ],
         out_specs=(anywhere, vmem),
@@ -409,6 +431,10 @@
             pltpu.VMEM((8, rows_here), F32),
             pltpu.VMEM((nz, 1, rows_here), F32),
             pltpu.VMEM((n, 1, rows_here), F32),
+            pltpu.VMEM((3, SHORT, channels), F32),
+            pltpu.VMEM((groups, MR), F32),
+            pltpu.VMEM((1, channels), F32),
+            dma((3,)),
             dma((channels // BLOCK, 3)),
             dma((2,)),
             dma((2,)),
@@ -420,7 +446,7 @@
             dma((n,)),
         ],
         compiler_params=pltpu.CompilerParams(
-            collective_id=0, has_side_effects=True, vmem_limit_bytes=40 * 1024 * 1024
+            collective_id=0, has_side_effects=True, vmem_limit_bytes=60 * 1024 * 1024
         ),
         cost_estimate=pl.CostEstimate(
             flops=channels * rows_here * 600, bytes_accessed=channels * rows_here * 8, transcendentals=0

time: 69.2 us -> 50.9 us (0.74)
  Pallas kernels: 58.3 us -> 46.4 us
  local copies, waits for them, and re-layouts: 8.61 us -> 0.76 us
  other arithmetic: 1.9 us -> 3.49 us
    pallas_call x1, Pallas kernels: 58.3 us -> 46.4 us  [local(): pl.pallas_call(functools.partial(kernel, n, nz), out_shape=(jax.ShapeDtyp...]
    unnamed x14 -> x0, local copies, waits for them, and re-layouts: 7.85 us -> none
    convert_element_type x1, other arithmetic: 1.9 us -> 3.49 us  [local(): return (received.astype(F32) * row_scale * gain_here[:, None]).astype(BF16)]
where the time goes in v2:
time: 50.9 us; the launch traced here: 50.7 us
  Pallas kernels  46.4 us (91%)
  other arithmetic  3.49 us (7%)
  local copies, waits for them, and re-layouts  0.76 us (1%)
    pallas_call x1, Pallas kernels, local(): pl.pallas_call(functools.partial(kernel, n, nz), out_shape=(jax.ShapeDtyp...  46.4 us
    convert_element_type x1, other arithmetic, local(): return (received.astype(F32) * row_scale * gain_here[:, None]).astype(BF16)  3.49 us

profile of v2, /device:TPU:0, one launch (start us, length us, event | category | flops | bytes accessed | tf_op | source)
XLA Modules:
  0.0 50.7 jit_solution(2727348501483374565)
XLA Ops:
  0.0 0.8 %dynamic_slice.3 = f32[256]{0:T(256)S(1)} dynamic-slice(f32[2048]{0:T(1024)} %param.14, s32[]{:T(128)S(6)} %select_n.3), dynamic_slice_sizes={256} | dynamic-slice | bytes 2052 | tf_op jit(solution)/shard_map/dynamic_slice | solution.py:463
  0.8 46.4 %shard_map.82 = (bf16[256,4096]{1,0:T(8,128)(2,1)}, f32[8,1,512]{2,1,0:T(1,128)}) custom-call(bf16[2048,512]{1,0:T(8,128)(2,1)} %gate_hbm.1, bf16[2048,512]{1,0:T(8,128)(2,1)} %key_hbm.1, bf16[2048,512]{1,0:T(8,128)(2,1)} %value_hbm.1, f32[3,3,2048]{2,1,0:T(4,128)} %sf_hbm.1, f32[128,128]{1,0:T(8,128)} %mr_hbm.1, f32[1,2048]{1,0:T(1,128)} %bitcast.3, s32[16]{0:T(128)} %docs_ref.1), custom_call_target="tpu_custom_call" | custom-call | flops 629145600 | bytes 8388608 | tf_op jit(solution)/shard_map/pallas_call | solution.py:403
  47.2 3.5 %multiply_convert_fusion = bf16[256,4096]{1,0:T(8,128)(2,1)} fusion(bf16[256,4096]{1,0:T(8,128)(2,1)} %get-tuple-element.7, f32[256]{0:T(256)S(1)} %dynamic_slice.3, f32[4096]{0:T(1024)} %bitcast.2), kind=kLoop, calls=%fused_computation | loop fusion | flops 4194304 | bytes 4211712 | tf_op jit(solution)/shard_map/convert_element_type | solution.py:465

commit v3 on v2

--- a/solution.py
+++ b/solution.py
@@ -14,7 +14,6 @@
 NORM_EPS = 1e-06
 
 LANES = 128
-BLOCK = 256
 F32 = jnp.float32
 BF16 = jnp.bfloat16
 
@@ -40,6 +39,7 @@
     sf_hbm,
     mr_hbm,
     skip_hbm,
+    gain_hbm,
     docs_ref,
     recv_ref,
     scale_ref,
@@ -60,6 +60,7 @@
     sf_ref,
     mr_ref,
     skip_ref,
+    gain_ref,
     small_sem,
     load_sem,
     halo_send,
@@ -77,13 +78,17 @@
     chunk = channels // n
     groups = channels // GROUP
     tiles = rows_here // LANES
-    blocks = channels // BLOCK
+    chunk_groups = chunk // GROUP
     barrier = pltpu.get_barrier_semaphore()
+
+    def offset(step):
+        odd = (step + n // 2 + 1) // n
+        return ((2 * (step + 1) + 3 * odd) % n) * (1 - (step + 1) // n)
 
     def load(b, which):
         source = (gate_hbm, key_hbm, value_hbm)[which]
         target = (g_ext, k_ext, v_ext)[which]
-        span = pl.ds(pl.multiple_of(b * BLOCK, BLOCK), BLOCK)
+        span = pl.ds(pl.multiple_of(b * chunk, chunk), chunk)
         return pltpu.make_async_copy(
             source.at[span, :],
             target.at[span, LANES : LANES + rows_here],
@@ -93,14 +98,15 @@
     small = [
         pltpu.make_async_copy(source, target, small_sem.at[i])
         for i, (source, target) in enumerate(
-            ((sf_hbm, sf_ref), (skip_hbm, skip_ref), (mr_hbm, mr_ref))
+            ((sf_hbm, sf_ref), (skip_hbm, skip_ref), (gain_hbm, gain_ref), (mr_hbm, mr_ref))
         )
     ]
     for copy in small:
         copy.start()
-    for b in range(blocks):
-        for which in range(3):
-            load(b, which).start()
+    for step in range(n):
+        dest = lax.rem(me + offset(step), n)
+        for which in (1, 2, 0):
+            load(dest, which).start()
     for k in range(1, n):
         pl.semaphore_signal(barrier, inc=1, device_id={"ctx": lax.rem(me + k, n)})
     for k in range(1, nz):
@@ -129,8 +135,8 @@
 
     for b in range(channels // LANES):
         span = slice(b * LANES, (b + 1) * LANES)
-        parts = [sf_ref[a, :, span] for a in range(3)] + [skip_ref[:, span]]
-        parts.append(jnp.zeros((6, LANES), F32))
+        parts = [sf_ref[a, :, span] for a in range(3)] + [skip_ref[:, span], gain_ref[:, span]]
+        parts.append(jnp.zeros((5, LANES), F32))
         coef[span, 0:16] = jnp.concatenate(parts, axis=0).T
 
     row16 = lax.broadcasted_iota(jnp.int32, (16, LANES), 0)
@@ -142,96 +148,65 @@
 
     last = tiles * LANES
 
-    def halo_block(b, carry):
-        for which in range(3):
-            load(b, which).wait()
-        span = pl.ds(pl.multiple_of(b * BLOCK, BLOCK), BLOCK)
-        columns = jnp.zeros((16, BLOCK), F32)
-        for which, ref in enumerate((g_ext, k_ext, v_ext)):
-            columns = columns + lax.dot_general(
-                pick(which),
-                ref[span, last : last + LANES],
-                (((1,), (1,)), ((), ())),
-                preferred_element_type=F32,
-            )
-        raw_send[:, span] = columns.astype(BF16)
-        m1 = lagmask[1:2, last - LANES : last]
-        m2 = lagmask[2:3, last - LANES : last]
-
-        def halo_rows(i, c):
-            rows = pl.ds(pl.multiple_of(b * BLOCK + i * 32, 32), 32)
-            kc = short_conv(k_ext, coef, rows, tiles - 1, 1, 1, m1, m2)
-            vc = short_conv(v_ext, coef, rows, tiles - 1, 1, 2, m1, m2)
-            p_ext[rows, last : last + LANES] = (kc * vc).astype(BF16)
-            return c
-
-        lax.fori_loop(0, BLOCK // 32, halo_rows, 0, unroll=4)
-        return carry
-
-    lax.fori_loop(0, blocks, halo_block, 0)
-
-    pl.semaphore_wait(barrier, n - 1 + nz - 1)
     right = lax.rem(me + 1, n)
 
-    def raw_copy():
+    def chunk_rows(c):
+        return pl.ds(pl.multiple_of(c * chunk, chunk), chunk)
+
+    def raw_copy(c):
         return pltpu.make_async_remote_copy(
-            src_ref=raw_send,
-            dst_ref=raw_recv,
-            send_sem=halo_send.at[0],
-            recv_sem=halo_recv.at[0],
+            src_ref=raw_send.at[c],
+            dst_ref=raw_recv.at[c],
+            send_sem=halo_send.at[c, 0],
+            recv_sem=halo_recv.at[c, 0],
             device_id={"ctx": right},
         )
 
-    def product_copy():
+    def product_copy(c):
         return pltpu.make_async_remote_copy(
-            src_ref=p_ext.at[:, last : last + LANES],
-            dst_ref=p_ext.at[:, 0:LANES],
-            send_sem=halo_send.at[1],
-            recv_sem=halo_recv.at[1],
+            src_ref=p_ext.at[chunk_rows(c), last : last + LANES],
+            dst_ref=p_ext.at[chunk_rows(c), 0:LANES],
+            send_sem=halo_send.at[c, 1],
+            recv_sem=halo_recv.at[c, 1],
             device_id={"ctx": right},
         )
-
-    @pl.when(me < n - 1)
-    def _():
-        raw_copy().start()
-        product_copy().start()
 
     @pl.when(me == 0)
     def _():
         raw_recv[...] = jnp.zeros(raw_recv.shape, BF16)
         p_ext[:, 0:LANES] = jnp.zeros((channels, LANES), BF16)
 
-    def build(g, carry):
-        taps = jnp.broadcast_to(mr_ref[pl.ds(g, 1), :], (LANES, LANES))
-        turned = pltpu.roll(taps, 0, 1, stride=1, stride_axis=0)
-        circ[g] = turned.astype(BF16)
-        return carry
-
-    @pl.when(me > 0)
-    def _():
-        raw_copy().wait_recv()
-
-    def spread(b, carry):
-        span = pl.ds(pl.multiple_of(b * BLOCK, BLOCK), BLOCK)
+    def take_raw(c):
+        columns = jnp.zeros((16, chunk), F32)
         for which, ref in enumerate((g_ext, k_ext, v_ext)):
-            ref[span, 0:LANES] = lax.dot_general(
-                raw_recv[:, span],
+            columns = columns + lax.dot_general(
+                pick(which),
+                ref[chunk_rows(c), last : last + LANES],
+                (((1,), (1,)), ((), ())),
+                preferred_element_type=F32,
+            )
+        raw_send[c] = columns.astype(BF16)
+
+    def spread_raw(c):
+        for which, ref in enumerate((g_ext, k_ext, v_ext)):
+            ref[chunk_rows(c), 0:LANES] = lax.dot_general(
+                raw_recv[c],
                 pick(which),
                 (((0,), (0,)), ((), ())),
                 preferred_element_type=F32,
             ).astype(BF16)
-        return carry
-
-    lax.fori_loop(0, blocks, spread, 0)
-
-    def products(i, carry):
-        rows = pl.ds(pl.multiple_of(i * GROUP, GROUP), GROUP)
-        m1 = lagmask[1:2, 0 : last - LANES]
-        m2 = lagmask[2:3, 0 : last - LANES]
-        kc = short_conv(k_ext, coef, rows, 0, tiles - 1, 1, m1, m2)
-        vc = short_conv(v_ext, coef, rows, 0, tiles - 1, 2, m1, m2)
-        p_ext[rows, LANES:last] = (kc * vc).astype(BF16)
-        return carry
+
+    def build(g):
+        taps = jnp.broadcast_to(mr_ref[pl.ds(g, 1), :], (LANES, LANES))
+        circ[g] = pltpu.roll(taps, 0, 1, stride=1, stride_axis=0).astype(BF16)
+
+    def products(g, first_tile, count):
+        rows = pl.ds(pl.multiple_of(g * GROUP, GROUP), GROUP)
+        lanes = slice(first_tile * LANES, (first_tile + count) * LANES)
+        m1, m2 = lagmask[1:2, lanes], lagmask[2:3, lanes]
+        kc = short_conv(k_ext, coef, rows, first_tile, count, 1, m1, m2)
+        vc = short_conv(v_ext, coef, rows, first_tile, count, 2, m1, m2)
+        p_ext[rows, (first_tile + 1) * LANES : (first_tile + 1 + count) * LANES] = (kc * vc).astype(BF16)
 
     acc[...] = jnp.zeros(acc.shape, F32)
 
@@ -256,12 +231,14 @@
             g_ext, coef, rows, first_tile, count, 0, lagmask[1:2, lanes], lagmask[2:3, lanes]
         )
         gated = gate * mixed
-        sendbuf[rows, lanes] = gated.astype(BF16)
+        sendbuf[rows, lanes] = (gated * coef[rows, 10:11]).astype(BF16)
         squares = gated * gated
         return squares[0:8] + squares[8:16]
 
+    late = (tiles // 2) * LANES
+
     def data_copy(dest, source, half):
-        lanes = (LANES, last - LANES) if half == 0 else (0, LANES)
+        lanes = (late, last - late) if half == 0 else (0, late)
         return pltpu.make_async_remote_copy(
             src_ref=sendbuf.at[
                 pl.ds(pl.multiple_of(dest * chunk, chunk), chunk), lanes[0] : lanes[0] + lanes[1]
@@ -275,7 +252,7 @@
         )
 
     def own_copy(half):
-        lanes = (LANES, last - LANES) if half == 0 else (0, LANES)
+        lanes = (late, last - late) if half == 0 else (0, late)
         return pltpu.make_async_copy(
             sendbuf.at[
                 pl.ds(pl.multiple_of(me * chunk, chunk), chunk), lanes[0] : lanes[0] + lanes[1]
@@ -284,30 +261,55 @@
             data_send.at[me, half],
         )
 
-    def stage(half, first_tile, count, together):
+    def stage(half, first_tile, count):
         lanes = slice(first_tile * LANES, (first_tile + count) * LANES)
-        chunk_groups = chunk // GROUP
+        together = min(16, chunk_groups)
+        unroll = min(8, chunk_groups)
 
         def one(step, carry):
-            k = lax.rem(step + 2, n)
+            k = offset(step)
             dest = lax.rem(me + k, n)
-
+            first_group = dest * chunk_groups
             if half == 0:
-                first = dest * chunk_groups
-                unroll = min(4, chunk_groups)
-                lax.fori_loop(
-                    0, chunk_groups, lambda i, c: build(first + i, c), 0, unroll=unroll
-                )
-                lax.fori_loop(
-                    0, chunk_groups, lambda i, c: products(first + i, c), 0, unroll=unroll
-                )
+                for which in (1, 2, 0):
+                    load(dest, which).wait()
+
+                def early(i, c):
+                    build(first_group + i)
+                    products(first_group + i, 1, tiles - 1)
+                    return c
+
+                lax.fori_loop(0, chunk_groups, early, 0, unroll=unroll)
+                take_raw(dest)
+
+                @pl.when(step == 0)
+                def _():
+                    pl.semaphore_wait(barrier, n - 1 + nz - 1)
+
+                @pl.when(me < n - 1)
+                def _():
+                    raw_copy(dest).start()
+                    product_copy(dest).start()
+
+            else:
+
+                @pl.when(me > 0)
+                def _():
+                    raw_copy(dest).wait_recv()
+                    product_copy(dest).wait_recv()
+
+                spread_raw(dest)
+
+                def rest(i, c):
+                    products(first_group + i, 0, 1)
+                    return c
+
+                lax.fori_loop(0, chunk_groups, rest, 0, unroll=unroll)
 
             def some(i, c):
                 total = jnp.zeros((8, count * LANES), F32)
                 for j in range(together):
-                    total = total + mix(
-                        dest * chunk_groups + i * together + j, first_tile, count
-                    )
+                    total = total + mix(first_group + i * together + j, first_tile, count)
                 acc[:, lanes] += total
                 return c
 
@@ -325,14 +327,8 @@
 
         lax.fori_loop(0, n, one, 0)
 
-    together = min(8, chunk // GROUP)
-    stage(0, 1, tiles - 1, together)
-
-    @pl.when(me > 0)
-    def _():
-        product_copy().wait_recv()
-
-    stage(1, 0, 1, together)
+    stage(0, tiles // 2, tiles - tiles // 2)
+    stage(1, 0, tiles // 2)
 
     sq_all[mz] = jnp.sum(acc[...], axis=0, keepdims=True)
 
@@ -385,8 +381,12 @@
 
     @pl.when(me < n - 1)
     def _():
-        raw_copy().wait_send()
-        product_copy().wait_send()
+        def sent(c, carry):
+            raw_copy(c).wait_send()
+            product_copy(c).wait_send()
+            return carry
+
+        lax.fori_loop(0, n, sent, 0)
 
 
 def local(
@@ -398,6 +398,7 @@
     tiles = rows_here // LANES
     ext = pltpu.VMEM((channels, rows_here + LANES), BF16)
     anywhere = pl.BlockSpec(memory_space=pl.ANY)
+    hbm = pl.BlockSpec(memory_space=pltpu.HBM)
     vmem = pl.BlockSpec(memory_space=pltpu.VMEM)
     dma = pltpu.SemaphoreType.DMA
     received, scales = pl.pallas_call(
@@ -406,15 +407,7 @@
             jax.ShapeDtypeStruct((chunk, n * rows_here), BF16),
             jax.ShapeDtypeStruct((n, 1, rows_here), F32),
         ),
-        in_specs=[
-            anywhere,
-            anywhere,
-            anywhere,
-            anywhere,
-            anywhere,
-            anywhere,
-            pl.BlockSpec(memory_space=pltpu.SMEM),
-        ],
+        in_specs=[hbm] * 7 + [pl.BlockSpec(memory_space=pltpu.SMEM)],
         out_specs=(anywhere, vmem),
         scratch_shapes=[
             ext,
@@ -426,18 +419,19 @@
             pltpu.VMEM((tiles, 2 * LANES, LANES), BF16),
             pltpu.VMEM((8, rows_here), F32),
             pltpu.VMEM((channels, rows_here), BF16),
-            pltpu.VMEM((16, channels), BF16),
-            pltpu.VMEM((16, channels), BF16),
+            pltpu.VMEM((n, 16, chunk), BF16),
+            pltpu.VMEM((n, 16, chunk), BF16),
             pltpu.VMEM((8, rows_here), F32),
             pltpu.VMEM((nz, 1, rows_here), F32),
             pltpu.VMEM((n, 1, rows_here), F32),
             pltpu.VMEM((3, SHORT, channels), F32),
             pltpu.VMEM((groups, MR), F32),
             pltpu.VMEM((1, channels), F32),
-            dma((3,)),
-            dma((channels // BLOCK, 3)),
-            dma((2,)),
-            dma((2,)),
+            pltpu.VMEM((1, channels), F32),
+            dma((4,)),
+            dma((n, 3)),
+            dma((n, 2)),
+            dma((n, 2)),
             dma((n, 2)),
             dma((n, 2)),
             dma((nz,)),
@@ -446,7 +440,7 @@
             dma((n,)),
         ],
         compiler_params=pltpu.CompilerParams(
-            collective_id=0, has_side_effects=True, vmem_limit_bytes=60 * 1024 * 1024
+            collective_id=0, has_side_effects=True, vmem_limit_bytes=56 * 1024 * 1024
         ),
         cost_estimate=pl.CostEstimate(
             flops=channels * rows_here * 600, bytes_accessed=channels * rows_here * 8, transcendentals=0
@@ -458,11 +452,11 @@
         short_filter,
         mr_filter,
         mr_skip.reshape(1, channels),
+        norm_gain.reshape(1, channels),
         doc_lengths,
     )
-    gain_here = lax.dynamic_slice_in_dim(norm_gain, lax.axis_index("ctx") * chunk, chunk)
     row_scale = scales.reshape(1, n * rows_here)
-    return (received.astype(F32) * row_scale * gain_here[:, None]).astype(BF16)
+    return (received.astype(F32) * row_scale).astype(BF16)
 
 
 def solution(mesh):

time: 50.9 us -> 46.4 us (0.912)
  Pallas kernels: 46.4 us -> 42.9 us
  local copies, waits for them, and re-layouts: 0.76 us -> 0 us
    pallas_call x1, Pallas kernels: 46.4 us -> 42.9 us  [local(): pl.pallas_call(functools.partial(kernel, n, nz), out_shape=(jax.ShapeDtyp...]
    dynamic_slice x1 -> x0, local copies, waits for them, and re-layouts: 0.76 us -> none  [local(): lax.dynamic_slice_in_dim(norm_gain, lax.axis_index('ctx') * chunk, chunk)]
where the time goes in v3:
time: 46.4 us; the launch traced here: 46.3 us
  Pallas kernels  42.9 us (92%)
  other arithmetic  3.38 us (7%)
    pallas_call x1, Pallas kernels, local(): pl.pallas_call(functools.partial(kernel, n, nz), out_shape=(jax.ShapeDtyp...  42.9 us
    convert_element_type x1, other arithmetic, local(): return (received.astype(F32) * row_scale).astype(BF16)  3.38 us

profile of v3, /device:TPU:0, one launch (start us, length us, event | category | flops | bytes accessed | tf_op | source)
XLA Modules:
  0.0 46.3 jit_solution(13744030753658568600)
XLA Ops:
  0.0 42.9 %shard_map.82 = (bf16[256,4096]{1,0:T(8,128)(2,1)}, f32[8,1,512]{2,1,0:T(1,128)}) custom-call(bf16[2048,512]{1,0:T(8,128)(2,1)} %gate_hbm.1, bf16[2048,512]{1,0:T(8,128)(2,1)} %key_hbm.1, bf16[2048,512]{1,0:T(8,128)(2,1)} %value_hbm.1, f32[3,3,2048]{2,1,0:T(4,128)} %sf_hbm.1, f32[128,128]{1,0:T(8,128)} %mr_hbm.1, f32[1,2048]{1,0:T(1,128)} %bitcast.4, ...), custom_call_target="tpu_custom_call" | custom-call | flops 629145600 | bytes 8388608 | tf_op jit(solution)/shard_map/pallas_call | solution.py:404
  42.9 3.4 %multiply_convert_fusion = bf16[256,4096]{1,0:T(8,128)(2,1)} fusion(bf16[256,4096]{1,0:T(8,128)(2,1)} %get-tuple-element.7, f32[4096]{0:T(1024)} %bitcast.3), kind=kLoop, calls=%fused_computation | loop fusion | flops 3145728 | bytes 4210688 | tf_op jit(solution)/shard_map/convert_element_type | solution.py:459

commit v4 on v3

--- a/solution.py
+++ b/solution.py
@@ -211,18 +211,20 @@
     acc[...] = jnp.zeros(acc.shape, F32)
 
     def mix(g, first_tile, count):
-        rows = pl.ds(pl.multiple_of(g * GROUP, GROUP), GROUP)
+        rows = pl.ds(pl.multiple_of(g * GROUP, 2 * GROUP), 2 * GROUP)
         lanes = slice(first_tile * LANES, (first_tile + count) * LANES)
-        c = circ[g]
-        pair = jnp.concatenate([c, c], axis=0)
+        both = jnp.concatenate([circ[g], circ[g + 1]], axis=1)
+        pair = jnp.concatenate([both, both], axis=0)
         parts = []
         for tile in range(first_tile, first_tile + count):
+            mask = masks[tile]
+            result = jnp.dot(
+                p_ext[rows, tile * LANES : (tile + 2) * LANES],
+                pair * jnp.concatenate([mask, mask], axis=1),
+                preferred_element_type=F32,
+            )
             parts.append(
-                jnp.dot(
-                    p_ext[rows, tile * LANES : (tile + 2) * LANES],
-                    pair * masks[tile],
-                    preferred_element_type=F32,
-                )
+                jnp.concatenate([result[:GROUP, :LANES], result[GROUP:, LANES:]], axis=0)
             )
         mixed = parts[0] if count == 1 else jnp.concatenate(parts, axis=1)
         direct = p_ext[rows, (first_tile + 1) * LANES : (first_tile + 1 + count) * LANES]
@@ -233,7 +235,7 @@
         gated = gate * mixed
         sendbuf[rows, lanes] = (gated * coef[rows, 10:11]).astype(BF16)
         squares = gated * gated
-        return squares[0:8] + squares[8:16]
+        return squares[0:8] + squares[8:16] + squares[16:24] + squares[24:32]
 
     late = (tiles // 2) * LANES
 
@@ -308,7 +310,7 @@
 
             def some(i, c):
                 total = jnp.zeros((8, count * LANES), F32)
-                for j in range(together):
+                for j in range(0, together, 2):
                     total = total + mix(first_group + i * together + j, first_tile, count)
                 acc[:, lanes] += total
                 return c
@@ -387,6 +389,25 @@
             return carry
 
         lax.fori_loop(0, n, sent, 0)
+
+
+def scale_kernel(source, scales, target, held, scaled, load_sem, store_sem):
+    n, _, width = scales.shape
+    parts = load_sem.shape[0]
+    height = source.shape[0] // parts
+    spans = [slice(i * height, (i + 1) * height) for i in range(parts)]
+    loads = [pltpu.make_async_copy(source.at[r], held.at[r], load_sem.at[i]) for i, r in enumerate(spans)]
+    stores = [pltpu.make_async_copy(scaled.at[r], target.at[r], store_sem.at[i]) for i, r in enumerate(spans)]
+    for load in loads:
+        load.start()
+    for load, store, rows in zip(loads, stores, spans):
+        load.wait()
+        for i in range(n):
+            lanes = slice(i * width, (i + 1) * width)
+            scaled[rows, lanes] = (held[rows, lanes].astype(F32) * scales[i]).astype(BF16)
+        store.start()
+    for store in stores:
+        store.wait()
 
 
 def local(
@@ -455,8 +476,19 @@
         norm_gain.reshape(1, channels),
         doc_lengths,
     )
-    row_scale = scales.reshape(1, n * rows_here)
-    return (received.astype(F32) * row_scale).astype(BF16)
+    return pl.pallas_call(
+        scale_kernel,
+        out_shape=jax.ShapeDtypeStruct(received.shape, BF16),
+        in_specs=[anywhere, vmem],
+        out_specs=anywhere,
+        scratch_shapes=[
+            pltpu.VMEM(received.shape, BF16),
+            pltpu.VMEM(received.shape, BF16),
+            dma((chunk // 32,)),
+            dma((chunk // 32,)),
+        ],
+        compiler_params=pltpu.CompilerParams(vmem_limit_bytes=56 * 1024 * 1024),
+    )(received, scales)
 
 
 def solution(mesh):

time: 46.4 us -> 46.3 us (level)
  other arithmetic: 3.38 us -> 0 us
  Pallas kernels: 42.9 us -> 46.1 us
    convert_element_type x1 -> x0, other arithmetic: 3.38 us -> none  [local(): return (received.astype(F32) * row_scale).astype(BF16)]
    pallas_call x0 -> x1, Pallas kernels: none -> 3.16 us  [local(): pl.pallas_call(scale_kernel, out_shape=jax.ShapeDtypeStruct(received.shap...]
where the time goes in v4:
time: 46.3 us; the launch traced here: 46.1 us
  Pallas kernels  46.1 us (100%)
    pallas_call x1, Pallas kernels, local(): pl.pallas_call(functools.partial(kernel, n, nz), out_shape=(jax.ShapeDtyp...  42.9 us
    pallas_call x1, Pallas kernels, local(): pl.pallas_call(scale_kernel, out_shape=jax.ShapeDtypeStruct(received.shap...  3.16 us

profile of v4, /device:TPU:0, one launch (start us, length us, event | category | flops | bytes accessed | tf_op | source)
XLA Modules:
  0.0 46.1 jit_solution(12804802351289639490)
XLA Ops:
  0.0 42.9 %shard_map.82 = (bf16[256,4096]{1,0:T(8,128)(2,1)}, f32[8,1,512]{2,1,0:T(1,128)}) custom-call(bf16[2048,512]{1,0:T(8,128)(2,1)} %gate_hbm.1, bf16[2048,512]{1,0:T(8,128)(2,1)} %key_hbm.1, bf16[2048,512]{1,0:T(8,128)(2,1)} %value_hbm.1, f32[3,3,2048]{2,1,0:T(4,128)} %sf_hbm.1, f32[128,128]{1,0:T(8,128)} %mr_hbm.1, f32[1,2048]{1,0:T(1,128)} %bitcast.2, ...), custom_call_target="tpu_custom_call" | custom-call | flops 629145600 | bytes 8388608 | tf_op jit(solution)/shard_map/pallas_call | solution.py:425
  42.9 3.2 %shard_map.83 = bf16[256,4096]{1,0:T(8,128)(2,1)} custom-call(bf16[256,4096]{1,0:T(8,128)(2,1)} %get-tuple-element.7.source, f32[8,1,512]{2,1,0:T(1,128)} %get-tuple-element.8.scales), custom_call_target="tpu_custom_call" | custom-call | tf_op jit(solution)/shard_map/pallas_call | solution.py:479

commit v5 on v4

--- a/solution.py
+++ b/solution.py
@@ -54,9 +54,11 @@
     sendbuf,
     raw_send,
     raw_recv,
+    halo_out,
+    halo_in,
     acc,
     sq_all,
-    sc_all,
+    own_scale,
     sf_ref,
     mr_ref,
     skip_ref,
@@ -164,8 +166,8 @@
 
     def product_copy(c):
         return pltpu.make_async_remote_copy(
-            src_ref=p_ext.at[chunk_rows(c), last : last + LANES],
-            dst_ref=p_ext.at[chunk_rows(c), 0:LANES],
+            src_ref=halo_out.at[chunk_rows(c)],
+            dst_ref=halo_in.at[chunk_rows(c)],
             send_sem=halo_send.at[c, 1],
             recv_sem=halo_recv.at[c, 1],
             device_id={"ctx": right},
@@ -174,7 +176,7 @@
     @pl.when(me == 0)
     def _():
         raw_recv[...] = jnp.zeros(raw_recv.shape, BF16)
-        p_ext[:, 0:LANES] = jnp.zeros((channels, LANES), BF16)
+        halo_in[...] = jnp.zeros(halo_in.shape, BF16)
 
     def take_raw(c):
         columns = jnp.zeros((16, chunk), F32)
@@ -206,7 +208,10 @@
         m1, m2 = lagmask[1:2, lanes], lagmask[2:3, lanes]
         kc = short_conv(k_ext, coef, rows, first_tile, count, 1, m1, m2)
         vc = short_conv(v_ext, coef, rows, first_tile, count, 2, m1, m2)
-        p_ext[rows, (first_tile + 1) * LANES : (first_tile + 1 + count) * LANES] = (kc * vc).astype(BF16)
+        result = (kc * vc).astype(BF16)
+        p_ext[rows, (first_tile + 1) * LANES : (first_tile + 1 + count) * LANES] = result
+        if first_tile + count == tiles:
+            halo_out[rows] = result[:, (count - 1) * LANES :]
 
     acc[...] = jnp.zeros(acc.shape, F32)
 
@@ -218,8 +223,12 @@
         parts = []
         for tile in range(first_tile, first_tile + count):
             mask = masks[tile]
+            if tile == 0:
+                window = jnp.concatenate([halo_in[rows], p_ext[rows, LANES : 2 * LANES]], axis=1)
+            else:
+                window = p_ext[rows, tile * LANES : (tile + 2) * LANES]
             result = jnp.dot(
-                p_ext[rows, tile * LANES : (tile + 2) * LANES],
+                window,
                 pair * jnp.concatenate([mask, mask], axis=1),
                 preferred_element_type=F32,
             )
@@ -233,34 +242,22 @@
             g_ext, coef, rows, first_tile, count, 0, lagmask[1:2, lanes], lagmask[2:3, lanes]
         )
         gated = gate * mixed
-        sendbuf[rows, lanes] = (gated * coef[rows, 10:11]).astype(BF16)
+        sendbuf[0 if first_tile else 1, rows] = (gated * coef[rows, 10:11]).astype(BF16)
         squares = gated * gated
         return squares[0:8] + squares[8:16] + squares[16:24] + squares[24:32]
 
-    late = (tiles // 2) * LANES
-
     def data_copy(dest, source, half):
-        lanes = (late, last - late) if half == 0 else (0, late)
         return pltpu.make_async_remote_copy(
-            src_ref=sendbuf.at[
-                pl.ds(pl.multiple_of(dest * chunk, chunk), chunk), lanes[0] : lanes[0] + lanes[1]
-            ],
-            dst_ref=recv_ref.at[
-                :, pl.ds(pl.multiple_of(source * rows_here + lanes[0], LANES), lanes[1])
-            ],
+            src_ref=sendbuf.at[half, chunk_rows(dest)],
+            dst_ref=recv_ref.at[source, half],
             send_sem=data_send.at[dest, half],
             recv_sem=data_recv.at[source, half],
             device_id={"ctx": dest},
         )
 
     def own_copy(half):
-        lanes = (late, last - late) if half == 0 else (0, late)
         return pltpu.make_async_copy(
-            sendbuf.at[
-                pl.ds(pl.multiple_of(me * chunk, chunk), chunk), lanes[0] : lanes[0] + lanes[1]
-            ],
-            recv_ref.at[:, pl.ds(pl.multiple_of(me * rows_here + lanes[0], LANES), lanes[1])],
-            data_send.at[me, half],
+            sendbuf.at[half, chunk_rows(me)], recv_ref.at[me, half], data_send.at[me, half]
         )
 
     def stage(half, first_tile, count):
@@ -350,12 +347,14 @@
     total = sq_all[0]
     for z in range(1, nz):
         total = total + sq_all[z]
-    sc_all[me] = lax.rsqrt(total / D + NORM_EPS)
+    own_scale[0] = lax.rsqrt(total / D + NORM_EPS)
+    keep_scale = pltpu.make_async_copy(own_scale.at[0], scale_ref.at[me], sc_send.at[me])
+    keep_scale.start()
 
     def sc_copy(dest, source):
         return pltpu.make_async_remote_copy(
-            src_ref=sc_all.at[me],
-            dst_ref=sc_all.at[source],
+            src_ref=own_scale.at[0],
+            dst_ref=scale_ref.at[source],
             send_sem=sc_send.at[dest],
             recv_sem=sc_recv.at[source],
             device_id={"ctx": dest},
@@ -365,7 +364,7 @@
         sc_copy(lax.rem(me + k, n), me).start()
     for k in range(1, n):
         sc_copy(me, lax.rem(me + k, n)).wait_recv()
-    scale_ref[...] = sc_all[...]
+    keep_scale.wait()
 
     def finish(k, carry):
         other = lax.rem(me + k, n)
@@ -391,21 +390,24 @@
         lax.fori_loop(0, n, sent, 0)
 
 
-def scale_kernel(source, scales, target, held, scaled, load_sem, store_sem):
-    n, _, width = scales.shape
-    parts = load_sem.shape[0]
-    height = source.shape[0] // parts
-    spans = [slice(i * height, (i + 1) * height) for i in range(parts)]
-    loads = [pltpu.make_async_copy(source.at[r], held.at[r], load_sem.at[i]) for i, r in enumerate(spans)]
-    stores = [pltpu.make_async_copy(scaled.at[r], target.at[r], store_sem.at[i]) for i, r in enumerate(spans)]
-    for load in loads:
-        load.start()
-    for load, store, rows in zip(loads, stores, spans):
-        load.wait()
-        for i in range(n):
-            lanes = slice(i * width, (i + 1) * width)
-            scaled[rows, lanes] = (held[rows, lanes].astype(F32) * scales[i]).astype(BF16)
-        store.start()
+def scale_kernel(source, scales_hbm, target, held, scaled, scales, scale_sem, load_sem, store_sem):
+    n, _, _, width = source.shape
+    fetch = pltpu.make_async_copy(scales_hbm, scales, scale_sem)
+    fetch.start()
+    loads, stores = [], []
+    for i in range(n):
+        lanes = slice(2 * i * width, 2 * (i + 1) * width)
+        loads.append(pltpu.make_async_copy(source.at[i], held.at[i], load_sem.at[i]))
+        stores.append(pltpu.make_async_copy(scaled.at[:, lanes], target.at[:, lanes], store_sem.at[i]))
+        loads[i].start()
+    fetch.wait()
+    for i in range(n):
+        loads[i].wait()
+        for half in range(2):
+            first = (2 * i + 1 - half) * width
+            scale = scales[i, :, (1 - half) * width : (2 - half) * width]
+            scaled[:, first : first + width] = (held[i, half].astype(F32) * scale).astype(BF16)
+        stores[i].start()
     for store in stores:
         store.wait()
 
@@ -420,16 +422,15 @@
     ext = pltpu.VMEM((channels, rows_here + LANES), BF16)
     anywhere = pl.BlockSpec(memory_space=pl.ANY)
     hbm = pl.BlockSpec(memory_space=pltpu.HBM)
-    vmem = pl.BlockSpec(memory_space=pltpu.VMEM)
     dma = pltpu.SemaphoreType.DMA
     received, scales = pl.pallas_call(
         functools.partial(kernel, n, nz),
         out_shape=(
-            jax.ShapeDtypeStruct((chunk, n * rows_here), BF16),
+            jax.ShapeDtypeStruct((n, 2, chunk, rows_here // 2), BF16),
             jax.ShapeDtypeStruct((n, 1, rows_here), F32),
         ),
         in_specs=[hbm] * 7 + [pl.BlockSpec(memory_space=pltpu.SMEM)],
-        out_specs=(anywhere, vmem),
+        out_specs=(anywhere, anywhere),
         scratch_shapes=[
             ext,
             ext,
@@ -439,12 +440,14 @@
             pltpu.VMEM((channels, LANES), F32),
             pltpu.VMEM((tiles, 2 * LANES, LANES), BF16),
             pltpu.VMEM((8, rows_here), F32),
-            pltpu.VMEM((channels, rows_here), BF16),
+            pltpu.VMEM((2, channels, rows_here // 2), BF16),
             pltpu.VMEM((n, 16, chunk), BF16),
             pltpu.VMEM((n, 16, chunk), BF16),
+            pltpu.VMEM((channels, LANES), BF16),
+            pltpu.VMEM((channels, LANES), BF16),
             pltpu.VMEM((8, rows_here), F32),
             pltpu.VMEM((nz, 1, rows_here), F32),
-            pltpu.VMEM((n, 1, rows_here), F32),
+            pltpu.VMEM((1, 1, rows_here), F32),
             pltpu.VMEM((3, SHORT, channels), F32),
             pltpu.VMEM((groups, MR), F32),
             pltpu.VMEM((1, channels), F32),
@@ -478,14 +481,16 @@
     )
     return pl.pallas_call(
         scale_kernel,
-        out_shape=jax.ShapeDtypeStruct(received.shape, BF16),
-        in_specs=[anywhere, vmem],
+        out_shape=jax.ShapeDtypeStruct((chunk, n * rows_here), BF16),
+        in_specs=[anywhere, anywhere],
         out_specs=anywhere,
         scratch_shapes=[
             pltpu.VMEM(received.shape, BF16),
-            pltpu.VMEM(received.shape, BF16),
-            dma((chunk // 32,)),
-            dma((chunk // 32,)),
+            pltpu.VMEM((chunk, n * rows_here), BF16),
+            pltpu.VMEM(scales.shape, F32),
+            dma(()),
+            dma((n,)),
+            dma((n,)),
         ],
         compiler_params=pltpu.CompilerParams(vmem_limit_bytes=56 * 1024 * 1024),
     )(received, scales)

time: 46.3 us -> 45.3 us (0.978)
  Pallas kernels: 46.1 us -> 45.1 us
    pallas_call x1, Pallas kernels: 42.9 us -> 42.4 us  [local(): pl.pallas_call(functools.partial(kernel, n, nz), out_shape=(jax.ShapeDtyp...]
where the time goes in v5:
time: 45.3 us; the launch traced here: 45.1 us
  Pallas kernels  45.1 us (100%)
    pallas_call x1, Pallas kernels, local(): pl.pallas_call(functools.partial(kernel, n, nz), out_shape=(jax.ShapeDtyp...  42.4 us
    pallas_call x1, Pallas kernels, local(): pl.pallas_call(scale_kernel, out_shape=jax.ShapeDtypeStruct((chunk, n * r...  2.77 us

profile of v5, /device:TPU:0, one launch (start us, length us, event | category | flops | bytes accessed | tf_op | source)
XLA Modules:
  0.0 45.1 jit_solution(10665391841058687928)
XLA Ops:
  0.0 42.4 %shard_map.82 = (bf16[8,2,256,256]{3,2,1,0:T(8,128)(2,1)}, f32[8,1,512]{2,1,0:T(1,128)}) custom-call(bf16[2048,512]{1,0:T(8,128)(2,1)} %gate_hbm.1, bf16[2048,512]{1,0:T(8,128)(2,1)} %key_hbm.1, bf16[2048,512]{1,0:T(8,128)(2,1)} %value_hbm.1, f32[3,3,2048]{2,1,0:T(4,128)} %sf_hbm.1, f32[128,128]{1,0:T(8,128)} %mr_hbm.1, f32[1,2048]{1,0:T(1,128)} %bitcast.2, ...), custom_call_target="tpu_custom_call" | custom-call | flops 629145600 | bytes 8388608 | tf_op jit(solution)/shard_map/pallas_call | solution.py:426
  42.4 2.8 %shard_map.83 = bf16[256,4096]{1,0:T(8,128)(2,1)} custom-call(bf16[8,2,256,256]{3,2,1,0:T(8,128)(2,1)} %get-tuple-element.7.source, f32[8,1,512]{2,1,0:T(1,128)} %get-tuple-element.8.scales_hbm), custom_call_target="tpu_custom_call" | custom-call | tf_op jit(solution)/shard_map/pallas_call | solution.py:482

commit v6 on v5

--- a/solution.py
+++ b/solution.py
@@ -122,24 +122,30 @@
         first = first + docs_ref[d]
     for lag in (1, 2):
         lagmask[lag : lag + 1, :] = jnp.where(positions - lag >= starts, 1.0, 0.0).astype(F32)
-    s_index = lax.broadcasted_iota(jnp.int32, (LANES, LANES), 0)
-    t_index = lax.broadcasted_iota(jnp.int32, (LANES, LANES), 1)
-    for tile in range(tiles):
-        start_row = starts[:, tile * LANES : (tile + 1) * LANES]
-        here = me * rows_here + tile * LANES + s_index
-        before = (t_index < s_index) & (here - LANES >= start_row)
-        within = (t_index >= s_index) & (here >= start_row)
-        masks[tile, 0:LANES, :] = jnp.where(before, 1.0, 0.0).astype(BF16)
-        masks[tile, LANES : 2 * LANES, :] = jnp.where(within, 1.0, 0.0).astype(BF16)
-
     for copy in small:
         copy.wait()
 
-    for b in range(channels // LANES):
-        span = slice(b * LANES, (b + 1) * LANES)
+    def make_masks():
+        s_index = lax.broadcasted_iota(jnp.int32, (LANES, LANES), 0)
+        t_index = lax.broadcasted_iota(jnp.int32, (LANES, LANES), 1)
+        for tile in range(tiles):
+            start_row = starts[:, tile * LANES : (tile + 1) * LANES]
+            here = me * rows_here + tile * LANES + s_index
+            before = (t_index < s_index) & (here - LANES >= start_row)
+            within = (t_index >= s_index) & (here >= start_row)
+            masks[tile, 0:LANES, :] = jnp.where(before, 1.0, 0.0).astype(BF16)
+            masks[tile, LANES : 2 * LANES, :] = jnp.where(within, 1.0, 0.0).astype(BF16)
+
+    def coefficients(first):
+        span = pl.ds(pl.multiple_of(first, LANES), LANES)
         parts = [sf_ref[a, :, span] for a in range(3)] + [skip_ref[:, span], gain_ref[:, span]]
         parts.append(jnp.zeros((5, LANES), F32))
         coef[span, 0:16] = jnp.concatenate(parts, axis=0).T
+
+    by_chunk = chunk % LANES == 0
+    if not by_chunk:
+        for b in range(channels // LANES):
+            coefficients(b * LANES)
 
     row16 = lax.broadcasted_iota(jnp.int32, (16, LANES), 0)
     lane16 = lax.broadcasted_iota(jnp.int32, (16, LANES), 1)
@@ -270,8 +276,11 @@
             dest = lax.rem(me + k, n)
             first_group = dest * chunk_groups
             if half == 0:
-                for which in (1, 2, 0):
-                    load(dest, which).wait()
+                if by_chunk:
+                    for b in range(chunk // LANES):
+                        coefficients(dest * chunk + b * LANES)
+                load(dest, 1).wait()
+                load(dest, 2).wait()
 
                 def early(i, c):
                     build(first_group + i)
@@ -279,6 +288,7 @@
                     return c
 
                 lax.fori_loop(0, chunk_groups, early, 0, unroll=unroll)
+                load(dest, 0).wait()
                 take_raw(dest)
 
                 @pl.when(step == 0)
@@ -289,6 +299,10 @@
                 def _():
                     raw_copy(dest).start()
                     product_copy(dest).start()
+
+                @pl.when(step == 0)
+                def _():
+                    make_masks()
 
             else:
 

time: 45.3 us -> 44.9 us (level)
  no operation moved by 1% of the time
where the time goes in v6:
time: 44.9 us; the launch traced here: 44.7 us
  Pallas kernels  44.7 us (100%)
    pallas_call x1, Pallas kernels, local(): pl.pallas_call(functools.partial(kernel, n, nz), out_shape=(jax.ShapeDtyp...  42 us
    pallas_call x1, Pallas kernels, local(): pl.pallas_call(scale_kernel, out_shape=jax.ShapeDtypeStruct((chunk, n * r...  2.77 us

profile of v6, /device:TPU:0, one launch (start us, length us, event | category | flops | bytes accessed | tf_op | source)
XLA Modules:
  0.0 44.7 jit_solution(16362061901757342055)
XLA Ops:
  0.0 42.0 %shard_map.82 = (bf16[8,2,256,256]{3,2,1,0:T(8,128)(2,1)}, f32[8,1,512]{2,1,0:T(1,128)}) custom-call(bf16[2048,512]{1,0:T(8,128)(2,1)} %gate_hbm.1, bf16[2048,512]{1,0:T(8,128)(2,1)} %key_hbm.1, bf16[2048,512]{1,0:T(8,128)(2,1)} %value_hbm.1, f32[3,3,2048]{2,1,0:T(4,128)} %sf_hbm.1, f32[128,128]{1,0:T(8,128)} %mr_hbm.1, f32[1,2048]{1,0:T(1,128)} %bitcast.2, ...), custom_call_target="tpu_custom_call" | custom-call | flops 629145600 | bytes 8388608 | tf_op jit(solution)/shard_map/pallas_call | solution.py:440
  42.0 2.8 %shard_map.83 = bf16[256,4096]{1,0:T(8,128)(2,1)} custom-call(bf16[8,2,256,256]{3,2,1,0:T(8,128)(2,1)} %get-tuple-element.7.source, f32[8,1,512]{2,1,0:T(1,128)} %get-tuple-element.8.scales_hbm), custom_call_target="tpu_custom_call" | custom-call | tf_op jit(solution)/shard_map/pallas_call | solution.py:496

commit v7 on v6

--- a/solution.py
+++ b/solution.py
@@ -291,11 +291,19 @@
                 load(dest, 0).wait()
                 take_raw(dest)
 
-                @pl.when(step == 0)
+                @pl.when(step == 1)
                 def _():
                     pl.semaphore_wait(barrier, n - 1 + nz - 1)
-
-                @pl.when(me < n - 1)
+                    held = lax.rem(me + offset(0), n)
+
+                    @pl.when(me < n - 1)
+                    def _():
+                        raw_copy(held).start()
+                        product_copy(held).start()
+
+                    data_copy(held, me, 0).start()
+
+                @pl.when((step > 0) & (me < n - 1))
                 def _():
                     raw_copy(dest).start()
                     product_copy(dest).start()
@@ -328,7 +336,7 @@
 
             lax.fori_loop(0, chunk_groups // together, some, 0)
 
-            @pl.when(k != 0)
+            @pl.when((k != 0) & ((step > 0) | (half == 1)))
             def _():
                 data_copy(dest, me, half).start()
 

time: 44.9 us -> 47 us (1.047)
  Pallas kernels: 44.7 us -> 46.8 us
    pallas_call x1, Pallas kernels: 42 us -> 44.1 us  [local(): pl.pallas_call(functools.partial(kernel, n, nz), out_shape=(jax.ShapeDtyp...]
where the time goes in v7:
time: 47 us; the launch traced here: 46.8 us
  Pallas kernels  46.8 us (100%)
    pallas_call x1, Pallas kernels, local(): pl.pallas_call(functools.partial(kernel, n, nz), out_shape=(jax.ShapeDtyp...  44.1 us
    pallas_call x1, Pallas kernels, local(): pl.pallas_call(scale_kernel, out_shape=jax.ShapeDtypeStruct((chunk, n * r...  2.77 us

profile of v7, /device:TPU:0, one launch (start us, length us, event | category | flops | bytes accessed | tf_op | source)
XLA Modules:
  0.0 46.8 jit_solution(7528170786086981362)
XLA Ops:
  0.0 44.1 %shard_map.82 = (bf16[8,2,256,256]{3,2,1,0:T(8,128)(2,1)}, f32[8,1,512]{2,1,0:T(1,128)}) custom-call(bf16[2048,512]{1,0:T(8,128)(2,1)} %gate_hbm.1, bf16[2048,512]{1,0:T(8,128)(2,1)} %key_hbm.1, bf16[2048,512]{1,0:T(8,128)(2,1)} %value_hbm.1, f32[3,3,2048]{2,1,0:T(4,128)} %sf_hbm.1, f32[128,128]{1,0:T(8,128)} %mr_hbm.1, f32[1,2048]{1,0:T(1,128)} %bitcast.2, ...), custom_call_target="tpu_custom_call" | custom-call | flops 629145600 | bytes 8388608 | tf_op jit(solution)/shard_map/pallas_call | solution.py:448
  44.1 2.8 %shard_map.83 = bf16[256,4096]{1,0:T(8,128)(2,1)} custom-call(bf16[8,2,256,256]{3,2,1,0:T(8,128)(2,1)} %get-tuple-element.7.source, f32[8,1,512]{2,1,0:T(1,128)} %get-tuple-element.8.scales_hbm), custom_call_target="tpu_custom_call" | custom-call | tf_op jit(solution)/shard_map/pallas_call | solution.py:504

commit v8 on v6

--- a/solution.py
+++ b/solution.py
@@ -252,24 +252,40 @@
         squares = gated * gated
         return squares[0:8] + squares[8:16] + squares[16:24] + squares[24:32]
 
-    def data_copy(dest, source, half):
+    pieces = (2 if chunk_groups >= 16 else 1, 1)
+
+    def data_copy(dest, source, half, piece):
+        height = chunk // pieces[half]
         return pltpu.make_async_remote_copy(
-            src_ref=sendbuf.at[half, chunk_rows(dest)],
-            dst_ref=recv_ref.at[source, half],
-            send_sem=data_send.at[dest, half],
-            recv_sem=data_recv.at[source, half],
+            src_ref=sendbuf.at[
+                half, pl.ds(pl.multiple_of(dest * chunk + piece * height, height), height)
+            ],
+            dst_ref=recv_ref.at[source, half, piece * height : (piece + 1) * height],
+            send_sem=data_send.at[dest, half, piece],
+            recv_sem=data_recv.at[source, half, piece],
             device_id={"ctx": dest},
         )
 
     def own_copy(half):
         return pltpu.make_async_copy(
-            sendbuf.at[half, chunk_rows(me)], recv_ref.at[me, half], data_send.at[me, half]
+            sendbuf.at[half, chunk_rows(me)], recv_ref.at[me, half], data_send.at[me, half, 0]
         )
 
     def stage(half, first_tile, count):
         lanes = slice(first_tile * LANES, (first_tile + count) * LANES)
-        together = min(16, chunk_groups)
-        unroll = min(8, chunk_groups)
+        piece_groups = chunk_groups // pieces[half]
+        together = min(16, piece_groups)
+        unroll = min(8, piece_groups)
+
+        def mix_piece(first_group):
+            def some(i, c):
+                total = jnp.zeros((8, count * LANES), F32)
+                for j in range(0, together, 2):
+                    total = total + mix(first_group + i * together + j, first_tile, count)
+                acc[:, lanes] += total
+                return c
+
+            lax.fori_loop(0, piece_groups // together, some, 0)
 
         def one(step, carry):
             k = offset(step)
@@ -281,28 +297,36 @@
                         coefficients(dest * chunk + b * LANES)
                 load(dest, 1).wait()
                 load(dest, 2).wait()
-
-                def early(i, c):
-                    build(first_group + i)
-                    products(first_group + i, 1, tiles - 1)
-                    return c
-
-                lax.fori_loop(0, chunk_groups, early, 0, unroll=unroll)
-                load(dest, 0).wait()
-                take_raw(dest)
-
-                @pl.when(step == 0)
-                def _():
-                    pl.semaphore_wait(barrier, n - 1 + nz - 1)
-
-                @pl.when(me < n - 1)
-                def _():
-                    raw_copy(dest).start()
-                    product_copy(dest).start()
-
-                @pl.when(step == 0)
-                def _():
-                    make_masks()
+                for piece in range(pieces[0]):
+                    piece_first = first_group + piece * piece_groups
+
+                    def early(i, c, piece_first=piece_first):
+                        build(piece_first + i)
+                        products(piece_first + i, 1, tiles - 1)
+                        return c
+
+                    lax.fori_loop(0, piece_groups, early, 0, unroll=unroll)
+                    if piece == 0:
+                        load(dest, 0).wait()
+
+                        @pl.when(step == 0)
+                        def _():
+                            pl.semaphore_wait(barrier, n - 1 + nz - 1)
+                            make_masks()
+
+                    if piece == pieces[0] - 1:
+                        take_raw(dest)
+
+                        @pl.when(me < n - 1)
+                        def _():
+                            raw_copy(dest).start()
+                            product_copy(dest).start()
+
+                    mix_piece(piece_first)
+
+                    @pl.when(k != 0)
+                    def _(piece=piece):
+                        data_copy(dest, me, 0, piece).start()
 
             else:
 
@@ -318,19 +342,11 @@
                     return c
 
                 lax.fori_loop(0, chunk_groups, rest, 0, unroll=unroll)
-
-            def some(i, c):
-                total = jnp.zeros((8, count * LANES), F32)
-                for j in range(0, together, 2):
-                    total = total + mix(first_group + i * together + j, first_tile, count)
-                acc[:, lanes] += total
-                return c
-
-            lax.fori_loop(0, chunk_groups // together, some, 0)
-
-            @pl.when(k != 0)
-            def _():
-                data_copy(dest, me, half).start()
+                mix_piece(first_group)
+
+                @pl.when(k != 0)
+                def _():
+                    data_copy(dest, me, 1, 0).start()
 
             @pl.when(k == 0)
             def _():
@@ -383,8 +399,9 @@
     def finish(k, carry):
         other = lax.rem(me + k, n)
         for half in (0, 1):
-            data_copy(me, other, half).wait_recv()
-            data_copy(other, me, half).wait_send()
+            for piece in range(pieces[half]):
+                data_copy(me, other, half, piece).wait_recv()
+                data_copy(other, me, half, piece).wait_send()
         sc_copy(other, me).wait_send()
         return carry
 
@@ -470,8 +487,8 @@
             dma((n, 3)),
             dma((n, 2)),
             dma((n, 2)),
-            dma((n, 2)),
-            dma((n, 2)),
+            dma((n, 2, 2)),
+            dma((n, 2, 2)),
             dma((nz,)),
             dma((nz,)),
             dma((n,)),

time: 44.9 us -> 45 us (level)
  no operation moved by 1% of the time
where the time goes in v8:
time: 45 us; the launch traced here: 44.9 us
  Pallas kernels  44.8 us (100%)
    pallas_call x1, Pallas kernels, local(): pl.pallas_call(functools.partial(kernel, n, nz), out_shape=(jax.ShapeDtyp...  42.1 us
    pallas_call x1, Pallas kernels, local(): pl.pallas_call(scale_kernel, out_shape=jax.ShapeDtypeStruct((chunk, n * r...  2.77 us

profile of v8, /device:TPU:0, one launch (start us, length us, event | category | flops | bytes accessed | tf_op | source)
XLA Modules:
  0.0 44.9 jit_solution(12253805128882434959)
XLA Ops:
  0.0 42.1 %shard_map.82 = (bf16[8,2,256,256]{3,2,1,0:T(8,128)(2,1)}, f32[8,1,512]{2,1,0:T(1,128)}) custom-call(bf16[2048,512]{1,0:T(8,128)(2,1)} %gate_hbm.1, bf16[2048,512]{1,0:T(8,128)(2,1)} %key_hbm.1, bf16[2048,512]{1,0:T(8,128)(2,1)} %value_hbm.1, f32[3,3,2048]{2,1,0:T(4,128)} %sf_hbm.1, f32[128,128]{1,0:T(8,128)} %mr_hbm.1, f32[1,2048]{1,0:T(1,128)} %bitcast.2, ...), custom_call_target="tpu_custom_call" | custom-call | flops 629145600 | bytes 8388608 | tf_op jit(solution)/shard_map/pallas_call | solution.py:457
  42.1 2.8 %shard_map.83 = bf16[256,4096]{1,0:T(8,128)(2,1)} custom-call(bf16[8,2,256,256]{3,2,1,0:T(8,128)(2,1)} %get-tuple-element.7.source, f32[8,1,512]{2,1,0:T(1,128)} %get-tuple-element.8.scales_hbm), custom_call_target="tpu_custom_call" | custom-call | tf_op jit(solution)/shard_map/pallas_call | solution.py:513

commit v9 on v6

--- a/solution.py
+++ b/solution.py
@@ -269,7 +269,7 @@
     def stage(half, first_tile, count):
         lanes = slice(first_tile * LANES, (first_tile + count) * LANES)
         together = min(16, chunk_groups)
-        unroll = min(8, chunk_groups)
+        unroll = min(16, chunk_groups)
 
         def one(step, carry):
             k = offset(step)

time: 44.9 us -> 44.2 us (0.984)
  Pallas kernels: 44.7 us -> 44 us
    pallas_call x1, Pallas kernels: 42 us -> 41.2 us  [local(): pl.pallas_call(functools.partial(kernel, n, nz), out_shape=(jax.ShapeDtyp...]
where the time goes in v9:
time: 44.2 us; the launch traced here: 44 us
  Pallas kernels  44 us (100%)
    pallas_call x1, Pallas kernels, local(): pl.pallas_call(functools.partial(kernel, n, nz), out_shape=(jax.ShapeDtyp...  41.2 us
    pallas_call x1, Pallas kernels, local(): pl.pallas_call(scale_kernel, out_shape=jax.ShapeDtypeStruct((chunk, n * r...  2.77 us

profile of v9, /device:TPU:0, one launch (start us, length us, event | category | flops | bytes accessed | tf_op | source)
XLA Modules:
  0.0 44.0 jit_solution(6242007731677499167)
XLA Ops:
  0.0 41.2 %shard_map.82 = (bf16[8,2,256,256]{3,2,1,0:T(8,128)(2,1)}, f32[8,1,512]{2,1,0:T(1,128)}) custom-call(bf16[2048,512]{1,0:T(8,128)(2,1)} %gate_hbm.1, bf16[2048,512]{1,0:T(8,128)(2,1)} %key_hbm.1, bf16[2048,512]{1,0:T(8,128)(2,1)} %value_hbm.1, f32[3,3,2048]{2,1,0:T(4,128)} %sf_hbm.1, f32[128,128]{1,0:T(8,128)} %mr_hbm.1, f32[1,2048]{1,0:T(1,128)} %bitcast.2, ...), custom_call_target="tpu_custom_call" | custom-call | flops 629145600 | bytes 8388608 | tf_op jit(solution)/shard_map/pallas_call | solution.py:440
  41.2 2.8 %shard_map.83 = bf16[256,4096]{1,0:T(8,128)(2,1)} custom-call(bf16[8,2,256,256]{3,2,1,0:T(8,128)(2,1)} %get-tuple-element.7.source, f32[8,1,512]{2,1,0:T(1,128)} %get-tuple-element.8.scales_hbm), custom_call_target="tpu_custom_call" | custom-call | tf_op jit(solution)/shard_map/pallas_call | solution.py:496
